TPU v7x, 32 devices: a whole 2x2x4 slice. The times are simulated.
32 devices in a mesh: grp: 1, lat: 32 (over z, y, x, core).
Axes of the slice: x: 2, y: 2, z: 4, core: 2. Of those that a mesh axis runs over, the one named last changes fastest.
Arguments:
- spectrum: bfloat16 [2688, 128, 256], P(('grp', 'lat')), may hold values from -6 to 6
- owners: int32 [384], P('lat'), may hold values from 0 to 383, each once
- legendre: bfloat16 [2688, 128, 640], P('lat'), may hold values from -0.25 to 0.25
- gauss_weights: float32 [640], replicated, may hold values from 0.5 to 2
Outputs:
- grid_values: bfloat16 [640, 2, 1536, 128], P(('grp', 'lat'))
- tendency: bfloat16 [2688, 128, 256], P(('grp', 'lat'))
Inputs may be any that keep to these rules, and one draw needn't show every extreme that they name: `owners`: each pair index appears once; pair p stands for the wavenumbers p and 767 - p.
All inputs are finite; a program needn't handle non-finite values.
Results may differ from a plain program's by a relative error of at most 0.0092.
Values may be sent and summed in bfloat16 or wider, within the bound.
A program may use at most 256 MiB of HBM per device.

v0:
```python
import math

import jax
import jax.numpy as jnp
from jax import lax
from jax.sharding import PartitionSpec as P

M = 768
BS = 128
NB = 6
NBP = 7
NLON = 1536


def block_layout(pair_ids):
    lowest = pair_ids // BS
    block_ids = jnp.arange(NBP, dtype=jnp.int32)
    leading = block_ids[None, :] < (NB - lowest)[:, None]
    wavenum = jnp.where(leading, pair_ids[:, None], M - 1 - pair_ids[:, None])
    nblock = jnp.where(leading, lowest[:, None] + block_ids[None, :], block_ids[None, :] - 1)
    half_rows = BS // 2
    row_ids = jnp.arange(BS, dtype=jnp.int32)
    odd_flag = (row_ids >= half_rows).astype(jnp.int32)
    degree = (
        nblock[:, :, None] * BS
        + 2 * (row_ids % half_rows)[None, None, :]
        + (wavenum[:, :, None] + odd_flag[None, None, :]) % 2
    )
    live_rows = degree >= wavenum[:, :, None]
    return (leading, live_rows)


def fourier_basis(pair_ids):
    wave_list = jnp.stack([pair_ids, M - 1 - pair_ids], axis=1).reshape(M)
    longitude = jnp.arange(NLON, dtype=jnp.int32)
    phase_idx = longitude[:, None] * wave_list[None, :] % NLON
    angles = phase_idx.astype(jnp.float32) * (2.0 * math.pi / NLON)
    scaled = jnp.stack([jnp.cos(angles), -jnp.sin(angles)], axis=-1) * (1.0 / math.sqrt(M))
    return scaled.astype(jnp.bfloat16).reshape(NLON, 2 * M)


def per_device(spectrum, owners, legendre, gauss_weights):
    pair_count = owners.shape[0]
    half_rows = BS // 2
    column_count = spectrum.shape[2]
    channels = column_count // 2
    levels = channels // 2
    lat_devices = lax.axis_size("lat")
    leading, live_rows = block_layout(owners)
    spec_four = spectrum.reshape(pair_count, NBP, BS, column_count)
    table_four = legendre.reshape(pair_count, NBP, BS, legendre.shape[2])
    lat_pairs = table_four.shape[3]
    pairs_here = lat_pairs // lat_devices
    masked = spec_four * live_rows[..., None].astype(jnp.bfloat16)
    even_part = jnp.einsum(
        "qjrl,qjrc->qjlc",
        table_four[:, :, :half_rows],
        masked[:, :, :half_rows],
        preferred_element_type=jnp.float32,
    )
    odd_part = jnp.einsum(
        "qjrl,qjrc->qjlc",
        table_four[:, :, half_rows:],
        masked[:, :, half_rows:],
        preferred_element_type=jnp.float32,
    )
    weight_one = leading.astype(jnp.float32)[:, :, None, None]
    symmetric = jnp.stack(
        [jnp.sum(even_part * weight_one, 1), jnp.sum(even_part * (1.0 - weight_one), 1)], 1
    )
    antisym = jnp.stack(
        [jnp.sum(odd_part * weight_one, 1), jnp.sum(odd_part * (1.0 - weight_one), 1)], 1
    )
    hemispheres = jnp.stack([symmetric + antisym, symmetric - antisym], 0).astype(jnp.bfloat16)
    outgoing = hemispheres.transpose(3, 0, 1, 2, 4).reshape(
        lat_devices, pairs_here, 2, 2 * pair_count, 2, channels
    )
    outgoing = outgoing.transpose(1, 0, 2, 3, 4, 5)
    all_owners = lax.all_gather(owners, "lat", axis=0, tiled=True)
    fourier_table = fourier_basis(all_owners)
    received = lax.all_to_all(outgoing, "lat", split_axis=1, concat_axis=3, tiled=True)
    local_pairs = received.shape[0]
    flattened = received.reshape(local_pairs * 2, 2 * M, channels)
    values = jnp.einsum("wk,bkc->bwc", fourier_table, flattened, preferred_element_type=jnp.float32)
    wind_u = values[..., :levels]
    wind_v = values[..., levels:]
    product = jnp.concatenate(
        [wind_u * wind_v, 0.5 * (wind_u * wind_u - wind_v * wind_v)], axis=-1
    ).astype(jnp.bfloat16)
    coeffs = jnp.einsum(
        "wk,bwc->bkc", fourier_table, product, preferred_element_type=jnp.float32
    ).astype(jnp.bfloat16)
    grid_part = values.astype(jnp.bfloat16).reshape(local_pairs, 2, NLON, channels)
    coeffs = coeffs.reshape(local_pairs, 2, M, 2, channels)
    arrived = lax.all_to_all(coeffs, "lat", split_axis=2, concat_axis=0, tiled=True)
    weights = gauss_weights[:, None, None, None]
    arrived_wide = arrived.astype(jnp.float32)
    sym_all = (weights * (arrived_wide[:, 0] + arrived_wide[:, 1])).astype(jnp.bfloat16)
    anti_all = (weights * (arrived_wide[:, 0] - arrived_wide[:, 1])).astype(jnp.bfloat16)
    sym_four = jnp.moveaxis(sym_all.reshape(lat_pairs, pair_count, 2, column_count), 0, 2)
    anti_four = jnp.moveaxis(anti_all.reshape(lat_pairs, pair_count, 2, column_count), 0, 2)
    chosen_sym = jnp.where(
        leading[:, :, None, None], sym_four[:, 0][:, None], sym_four[:, 1][:, None]
    )
    chosen_anti = jnp.where(
        leading[:, :, None, None], anti_four[:, 0][:, None], anti_four[:, 1][:, None]
    )
    even_rows = jnp.einsum(
        "qjrl,qjlc->qjrc",
        table_four[:, :, :half_rows],
        chosen_sym,
        preferred_element_type=jnp.float32,
    )
    odd_rows = jnp.einsum(
        "qjrl,qjlc->qjrc",
        table_four[:, :, half_rows:],
        chosen_anti,
        preferred_element_type=jnp.float32,
    )
    combined = jnp.concatenate([even_rows, odd_rows], axis=2) * live_rows[..., None].astype(
        jnp.float32
    )
    tendency = combined.astype(jnp.bfloat16).reshape(pair_count * NBP, BS, column_count)
    return (grid_part, tendency)


def solution(mesh):
    in_specs = (P(("grp", "lat"), None, None), P("lat"), P("lat", None, None), P())
    out_specs = (P(("grp", "lat"), None, None, None), P(("grp", "lat"), None, None))
    return jax.shard_map(
        per_device, mesh=mesh, in_specs=in_specs, out_specs=out_specs, check_vma=False
    )
```

profile of v0, /device:TPU:0, one launch (start us, length us, event | category | flops | bytes accessed | tf_op | source)
XLA Modules:
  0.0 1216.1 jit_solution(9905974557205570130)
XLA Ops:
  0.7 0.7 broadcast_subtract_fusion.3
  1.3 0.7 iota_compare_fusion
  2.1 0.7 select_multiply_fusion
  2.8 0.1 fusion.39
  3.0 0.5 copy-done.1
  3.4 4.1 broadcast_multiply_fusion
  7.5 24.2 %fusion.24 = f32[12,7,256,640]{3,2,1,0:T(8,128)} fusion(bf16[12,7,128,640]{3,2,1,0:T(8,128)(2,1)} %bitcast.82, bf16[12,7,128,256]{3,2,1,0:T(8,128)(2,1)S(1)} %broadcast_multiply_fusion), kind=kOutput, calls=%fused_computation.43 | convolution fusion | flops 1761607680 | bytes 64684032 | tf_op jit(solution)/shard_map/qjrl,qjrc->qjlc/dot_general | solution.py:55
  31.8 42.6 %multiply_reduce_fusion.1 = (f32[12,256,640]{2,1,0:T(8,128)}, f32[12,256,640]{2,1,0:T(8,128)}, f32[12,256,640]{2,1,0:T(8,128)}, f32[12,256,640]{2,1,0:T(8,128)}) fusion(f32[12,7]{1,0:T(8,128)S(1)} %get-tuple-element.35, f32[12,7]{1,0:T(8,128)S(1)} %broadcast_subtract_fusion, f32[12,7,256,640]{3,2,1,0:T(8,128)} %fusion.24, ...), kind=kOutput, calls=%fused_computation.1 | convolution fusion | flops 1863843840 | bytes 96141984 | tf_op jit(solution)/shard_map/qjrl,qjrc->qjlc/dot_general | solution.py:61
  74.4 11.1 add_convert_fusion
  85.5 6.6 maximum_bitcast_fusion
  92.1 21.1 %copy.55 = bf16[640,2,12,2,256]{4,0,3,2,1:T(8,128)(2,1)} copy(bf16[640,2,12,2,256]{0,4,2,3,1:T(8,128)(2,1)} %maximum_bitcast_fusion) | data formatting | bytes 31457280 | tf_op jit(solution)/shard_map/transpose | solution.py:75
  113.2 22.3 %reshape.497 = bf16[32,20,2,24,2,128]{5,4,1,0,3,2:T(2,128)(2,1)} reshape(bf16[640,2,12,2,256]{4,0,3,2,1:T(8,128)(2,1)} %copy.55) | data formatting | bytes 31457280 | tf_op jit(solution)/shard_map/reshape | solution.py:75
  135.5 19.6 %copy.56 = bf16[20,32,2,24,2,128]{5,4,0,3,2,1:T(2,128)(2,1)} copy(bf16[20,32,2,24,2,128]{5,4,0,1,3,2:T(2,128)(2,1)} %bitcast.70) | data formatting | bytes 31457280 | tf_op jit(solution)/shard_map/transpose | solution.py:78
  155.2 7.4 all-to-all-start
  162.6 0.2 dynamic-update-slice
  162.8 368.5 %all-reduce = s32[384]{0:T(512)S(1)} all-reduce(s32[384]{0:T(512)S(1)} %dynamic-update-slice), channel_id=1, replica_groups=mesh['grp'=1,'lat'=32] {'lat'}, use_global_device_ids=true, to_apply=%add | all-reduce | flops 384 | bytes 3072
  531.4 0.1 copy.58
  531.5 0.1 mul.179
  531.7 19.2 %fusion.32 = (f32[1536,768,1]{1,0,2:T(8,128)S(1)}, f32[1536,768,1]{1,0,2:T(8,128)S(1)}) fusion(s32[768]{0:T(1024)S(1)} %mul.179), kind=kLoop, calls=%fused_computation.53 | loop fusion | flops 11796480 | bytes 9440256 | tf_op jit(solution)/shard_map/cos | solution.py:38
  550.9 3.3 fusion.17
  554.2 23.4 %copy.59 = bf16[1536,768,2]{0,2,1:T(2,128)(2,1)} copy(bf16[1536,768,2]{1,0,2:T(8,128)(2,1)} %fusion.17) | data formatting | bytes 9437184 | tf_op jit(solution)/shard_map/convert_element_type | solution.py:39
  577.6 10.7 convert_element_type.103
  588.3 12.9 %copy.57 = bf16[20,1,2,32,24,2,128]{6,5,4,3,2,0,1:T(2,128)(2,1)S(1)} copy(bf16[20,1,2,32,24,2,128]{6,5,0,4,2,3,1:T(2,128)(2,1)} %bitcast.13) | data formatting | bytes 31457280 | tf_op jit(solution)/shard_map/all_to_all | solution.py:81
  601.2 32.1 %fusion.48 = (bf16[40,1536,128]{1,2,0:T(8,128)(2,1)}, f32[40,1536,128]{1,2,0:T(8,128)}) fusion(bf16[40,1536,128]{2,1,0:T(8,128)(2,1)S(1)} %bitcast.74, bf16[1536,1536]{0,1:T(8,128)(2,1)} %convert_element_type.103), kind=kOutput, calls=%fused_computation.98 | convolution fusion | flops 24167055360 | bytes 67633152 | tf_op jit(solution)/shard_map/wk,bkc->bwc/dot_general | solution.py:84
  633.3 14.0 %multiply_convert_fusion.3 = (bf16[40,1536,64]{1,2,0:T(8,128)(2,1)S(1)}, bf16[40,1536,64]{1,2,0:T(8,128)(2,1)}) fusion(f32[40,1536,128]{1,2,0:T(8,128)} %get-tuple-element.40), kind=kLoop, calls=%fused_computation.23 | loop fusion | flops 27525120 | bytes 47185920 | tf_op jit(solution)/shard_map/convert.3
  647.3 29.7 %convert_bitcast_fusion.1 = bf16[40,1536,128]{1,2,0:T(8,128)(2,1)} fusion(bf16[40,1536,64]{1,2,0:T(8,128)(2,1)} %get-tuple-element.23, bf16[40,1536,64]{1,2,0:T(8,128)(2,1)S(1)} %get-tuple-element.22, bf16[1536,1536]{0,1:T(8,128)(2,1)} %convert_element_type.103), kind=kOutput, calls=%fused_computation.21 | convolution fusion | flops 24198512640 | bytes 36175872 | tf_op jit(solution)/shard_map/wk,bwc->bkc/dot_general | solution.py:90
  677.0 20.4 %copy.63 = bf16[40,1536,128]{2,1,0:T(8,128)(2,1)} copy(bf16[40,1536,128]{1,2,0:T(8,128)(2,1)} %convert_bitcast_fusion.1) | data formatting | bytes 31457280 | tf_op jit(solution)/shard_map/convert_element_type | solution.py:92
  697.4 13.8 %copy.64 = bf16[20,2,768,2,128]{4,3,1,0,2:T(2,128)(2,1)} copy(bf16[20,2,768,2,128]{4,3,2,1,0:T(2,128)(2,1)} %bitcast.71) | data formatting | bytes 31457280 | tf_op jit(solution)/shard_map/reshape | solution.py:94
  711.2 4.7 all-to-all-start.1
  716.0 0.1 mul.194
  716.2 0.1 fusion.43
  716.3 20.6 %copy.73 = bf16[20,2,1536,128]{3,2,1,0:T(8,128)(2,1)} copy(bf16[20,2,1536,128]{2,3,1,0:T(8,128)(2,1)} %bitcast.73) | data formatting | bytes 31457280
  736.8 328.4 %all-to-all-done.1 = bf16[20,2,768,2,128]{4,3,1,0,2:T(2,128)(2,1)} async-done(((bf16[20,2,768,2,128]{4,3,1,0,2:T(2,128)(2,1)}), bf16[20,2,768,2,128]{4,3,1,0,2:T(2,128)(2,1)}, u32[]{:S(2)}, u32[]{:S(2)}) %all-to-all-start.1) | async-done | bytes 15728672 | tf_op jit(solution)/shard_map/all_to_all | solution.py:95
  1065.2 14.7 %copy.65 = bf16[20,2,768,2,128]{4,2,3,1,0:T(8,128)(2,1)} copy(bf16[20,2,768,2,128]{4,3,1,0,2:T(2,128)(2,1)} %all-to-all-done.1) | data formatting | bytes 31457280 | tf_op jit(solution)/shard_map/all_to_all | solution.py:95
  1079.9 8.6 convert_bitcast_fusion
  1088.5 11.1 copy.66
  1099.6 21.0 %slice_add_fusion = (f32[640,1,24,2,128]{4,2,3,1,0:T(8,128)}, f32[640,1,24,2,128]{4,2,3,1,0:T(8,128)}) fusion(f32[640,2,24,2,128]{4,2,3,1,0:T(8,128)} %bitcast.67), kind=kLoop, calls=%fused_computation.27 | loop fusion | flops 7864320 | bytes 62914560 | tf_op jit(solution)/shard_map/add | solution.py:98
  1120.6 15.9 %copy.67 = f32[640,1,24,2,128]{0,4,3,2,1:T(8,128)} copy(f32[640,1,24,2,128]{4,2,3,1,0:T(8,128)} %get-tuple-element.20) | data formatting | bytes 31457280 | tf_op jit(solution)/shard_map/add | solution.py:98
  1136.5 15.9 %copy.70 = f32[640,1,24,2,128]{0,4,3,2,1:T(8,128)} copy(f32[640,1,24,2,128]{4,2,3,1,0:T(8,128)} %get-tuple-element.21) | data formatting | bytes 31457280 | tf_op jit(solution)/shard_map/sub | solution.py:99
  1152.5 11.0 fusion.18
  1163.5 5.8 slice_bitcast_fusion.1
  1169.2 6.3 copy.68
  1175.5 6.2 copy.69
  1181.8 6.3 copy.71
  1188.0 6.3 copy.72
  1194.3 8.9 fusion.2
  1203.2 8.9 fusion
  1212.1 3.7 fusion.16
  (34 shorter events, 0.3 us)
Async XLA Ops:
  0.7 2.3 copy-start.6
  0.7 2.3 copy-start.8
  2.8 0.6 copy-start.1
  2.8 0.6 copy-start.3
  7.5 24.2 %copy-start = (bf16[12,7,128,256]{3,2,1,0:T(8,128)(2,1)}, bf16[12,7,128,256]{3,2,1,0:T(8,128)(2,1)S(1)}, u32[]{:S(2)}) copy-start(bf16[12,7,128,256]{3,2,1,0:T(8,128)(2,1)S(1)} %broadcast_multiply_fusion) | copy-start | bytes 16515076
  155.2 7.4 copy-start.10
  155.2 433.1 %all-to-all-start = ((bf16[20,32,2,24,2,128]{5,4,0,3,2,1:T(2,128)(2,1)}), bf16[20,32,2,24,2,128]{5,4,0,3,2,1:T(2,128)(2,1)}, u32[]{:S(2)}, u32[]{:S(2)}) async-start(bf16[20,32,2,24,2,128]{5,4,0,3,2,1:T(2,128)(2,1)} %copy.56), calls=%async_computation | async-start | bytes 31457280 | tf_op jit(solution)/shard_map/all_to_all | solution.py:81
  711.2 4.8 copy-start.4
  711.2 4.9 copy-start.2
  711.2 4.9 copy-start.7
  711.2 4.9 copy-start.9
  711.2 354.0 %all-to-all-start.1 = ((bf16[20,2,768,2,128]{4,3,1,0,2:T(2,128)(2,1)}), bf16[20,2,768,2,128]{4,3,1,0,2:T(2,128)(2,1)}, u32[]{:S(2)}, u32[]{:S(2)}) async-start(bf16[20,2,768,2,128]{4,3,1,0,2:T(2,128)(2,1)} %copy.64), calls=%async_computation.1 | async-start | bytes 31457280 | tf_op jit(solution)/shard_map/all_to_all | solution.py:95
  1136.5 15.9 %copy-start.5 = (f32[640]{0:T(1024)S(1)}, f32[640]{0:T(1024)}, u32[]{:S(2)}) copy-start(f32[640]{0:T(1024)} %param.7) | copy-start | bytes 7684
  1181.8 12.6 %copy-start.11 = (pred[12,7]{1,0:T(8,128)(4,1)S(1)}, pred[12,7]{1,0:T(8,128)(4,1)}, u32[]{:S(2)}) copy-start(pred[12,7]{1,0:T(8,128)(4,1)} %get-tuple-element.34) | copy-start | bytes 256
where the time goes:
time: 1230 us; the launch traced here: 1220 us
  blocking collectives  369 us (30%)
  waiting for transfers between devices  328 us (27%)
  local copies, waits for them, and re-layouts  255 us (21%)
  matrix products  146 us (12%)
  other arithmetic  105 us (9%)
    unnamed x1, blocking collectives  369 us
    all_to_all x1, waiting for transfers between devices, per_device(): lax.all_to_all(coeffs, 'lat', split_axis=2, concat_axis=0, tiled=True)  328 us
    dot_general x1, matrix products, per_device(): jnp.einsum('qjrl,qjrc->qjlc', table_four[:, :, half_rows:], masked[:, :,...  42.6 us
    convert_element_type x2, local copies, waits for them, and re-layouts, fourier_basis(): return scaled.astype(jnp.bfloat16).reshape(NLON, 2 * M)  34.1 us
    dot_general x1, matrix products, per_device(): jnp.einsum('wk,bkc->bwc', fourier_table, flattened, preferred_element_typ...  32.1 us
    dot_general x1, matrix products, per_device(): jnp.einsum('wk,bwc->bkc', fourier_table, product, preferred_element_type=...  29.7 us
    another operation x2, other arithmetic  25.1 us
  transfers between devices with their start and end apart: 2, of which 1 were waited for; matrix products, arithmetic and copies ran while one was open for 6% of the time, Pallas kernels for 0%

commit v1 on v0

v1 whole, which is shorter than its diff:
```python
import functools
import math

import jax
import jax.numpy as jnp
from jax import lax
from jax.experimental import pallas as pl
from jax.experimental.pallas import tpu as pltpu
from jax.sharding import PartitionSpec as P

BF = jnp.bfloat16
F32 = jnp.float32
CHUNKS = 5


def dot(a, b, dims):
    return lax.dot_general(a, b, (dims, ((), ())), preferred_element_type=F32)


def params(mib):
    return pltpu.CompilerParams(vmem_limit_bytes=mib * 1024 * 1024)


def block_facts(p, j, nb, bs, m_count, shape):
    k = p // bs
    lead = j < nb - k
    m = jnp.where(lead, p, m_count - 1 - p)
    b = jnp.where(lead, k + j, j - 1)
    r = lax.broadcasted_iota(jnp.int32, shape, 0)
    half = bs // 2
    odd = (r >= half).astype(jnp.int32)
    degree = b * bs + 2 * (r % half) + ((m + odd) & 1)
    return lead, degree >= m


def inverse_kernel(dims, owners_ref, leg_ref, spec_ref, out_ref, acc_ref):
    nbp, bs, nb, m_count, rows, stride, chan = dims
    q = pl.program_id(0)
    half = bs // 2
    p = owners_ref[q]
    firsts, seconds = [], []
    for j in range(nbp):
        s = spec_ref[j].astype(F32)
        lead, live = block_facts(p, j, nb, bs, m_count, s.shape)
        one = lead.astype(F32)
        s = jnp.where(live, s, 0.0)
        both = jnp.concatenate([s * one, s * (1.0 - one)], axis=1).astype(BF)
        firsts.append(both[:half])
        seconds.append(both[half:])
    te = jnp.concatenate([leg_ref[j, :half] for j in range(nbp)], axis=0)
    to = jnp.concatenate([leg_ref[j, half:] for j in range(nbp)], axis=0)
    sym = dot(te, jnp.concatenate(firsts, axis=0), ((0,), (0,)))
    anti = dot(to, jnp.concatenate(seconds, axis=0), ((0,), (0,)))
    lats = sym.shape[0]
    for h, val in enumerate((sym + anti, sym - anti)):
        for x in range(4):
            acc_ref[h, pl.ds(q * 4 + x, lats, stride=stride), :] = val[:, x * chan:(x + 1) * chan]

    @pl.when(q == pl.num_programs(0) - 1)
    def _():
        for h in range(2):
            full = acc_ref[h].reshape(lats, stride, chan)
            out_ref[:, :, h * chan:(h + 1) * chan] = full[:, :rows].astype(BF)


def inverse(owners, leg, spec, chunk, lats, dims):
    nbp, bs, nb, m_count, rows, stride, chan = dims
    pairs = owners.shape[0]
    return pl.pallas_call(
        functools.partial(inverse_kernel, dims),
        grid_spec=pltpu.PrefetchScalarGridSpec(
            num_scalar_prefetch=1,
            grid=(pairs,),
            in_specs=[
                pl.BlockSpec((nbp, bs, lats), lambda q, o: (q, 0, chunk)),
                pl.BlockSpec((nbp, bs, 2 * chan), lambda q, o: (q, 0, 0)),
            ],
            out_specs=pl.BlockSpec((lats, rows, 2 * chan), lambda q, o: (0, 0, 0)),
            scratch_shapes=[pltpu.VMEM((2, lats * stride, chan), F32)],
        ),
        out_shape=jax.ShapeDtypeStruct((lats, rows, 2 * chan), BF),
        compiler_params=params(48),
        cost_estimate=pl.CostEstimate(flops=4 * 10**9, bytes_accessed=15 * 10**6, transcendentals=0),
        name="inverse_legendre",
    )(owners, leg, spec)


def fourier_kernel(chan, table_ref, turned_ref, recv_ref, prev_ref, grid_ref, send_ref):
    groups, _, rows, cols = recv_ref.shape
    total = groups * rows
    f = recv_ref[:, 0].reshape(total, cols)
    nlon = table_ref.shape[0]
    step = nlon // 4
    fluxes = []
    for w in range(4):
        values = dot(table_ref[w * step:(w + 1) * step], f, ((1,), (0,)))
        parts = []
        for h in range(2):
            x = values[:, h * chan:(h + 1) * chan]
            grid_ref[0, h, w * step:(w + 1) * step, :] = x.astype(BF)
            y = pltpu.roll(x, chan // 2, 1)
            lane = lax.broadcasted_iota(jnp.int32, x.shape, 1)
            parts.append(jnp.where(lane < chan // 2, x * y, 0.5 * (y * y - x * x)).astype(BF))
        fluxes.append(jnp.concatenate(parts, axis=1))
    flux = jnp.concatenate(fluxes, axis=0)
    coeffs = dot(turned_ref[...], flux, ((1,), (0,))).astype(BF)
    send_ref[:, 0] = coeffs.reshape(groups, rows, cols)


def fourier(table, turned, recv, prev, chunk, grid_shape):
    groups, lats, rows, cols = recv.shape
    nlon, total = table.shape
    chan = cols // 2
    whole = pl.BlockSpec((nlon, total), lambda t: (0, 0))
    turned_spec = pl.BlockSpec((total, nlon), lambda t: (0, 0))
    part = pl.BlockSpec((groups, 1, rows, cols), lambda t: (0, t, 0, 0))
    in_specs = [whole, turned_spec, part]
    args = [table, turned, recv]
    kernel = functools.partial(fourier_kernel, chan)
    alias = {}
    if prev is None:
        def kernel(a, b, c, d, e):
            fourier_kernel(chan, a, b, c, None, d, e)
    else:
        in_specs.append(pl.BlockSpec(memory_space=pl.ANY))
        args.append(prev)
        alias = {3: 0}
    return pl.pallas_call(
        kernel,
        grid=(lats,),
        in_specs=in_specs,
        out_specs=[
            pl.BlockSpec((1, 2, nlon, chan), lambda t: (chunk * lats + t, 0, 0, 0)),
            part,
        ],
        out_shape=[
            jax.ShapeDtypeStruct(grid_shape, BF),
            jax.ShapeDtypeStruct(recv.shape, BF),
        ],
        input_output_aliases=alias,
        compiler_params=params(56),
        cost_estimate=pl.CostEstimate(flops=4 * lats * nlon * total * cols, bytes_accessed=20 * 10**6, transcendentals=0),
        name="fourier_step",
    )(*args)


def direct_kernel(dims, first, last, owners_ref, leg_ref, gauss_ref, got_ref, *rest):
    nbp, bs, nb, m_count, rows, stride, chan = dims
    prev_ref = None if first else rest[0]
    out_ref, acc_ref = rest[-2:]
    q = pl.program_id(0)
    half = bs // 2
    p = owners_ref[q]
    lats = got_ref.shape[0]

    @pl.when(q == 0)
    def _():
        for h in range(2):
            full = got_ref[:, :, h * chan:(h + 1) * chan].astype(F32)
            if stride != rows:
                full = jnp.concatenate([full, jnp.zeros((lats, stride - rows, chan), F32)], axis=1)
            acc_ref[h] = full.reshape(lats * stride, chan)

    g = gauss_ref[...]
    syms, antis = [], []
    for x in range(4):
        north = acc_ref[0, pl.ds(q * 4 + x, lats, stride=stride), :]
        south = acc_ref[1, pl.ds(q * 4 + x, lats, stride=stride), :]
        syms.append((g * (north + south)).astype(BF))
        antis.append((g * (north - south)).astype(BF))
    te = jnp.concatenate([leg_ref[j, :half] for j in range(nbp)], axis=0)
    to = jnp.concatenate([leg_ref[j, half:] for j in range(nbp)], axis=0)
    even = dot(te, jnp.concatenate(syms, axis=1), ((1,), (0,)))
    odd = dot(to, jnp.concatenate(antis, axis=1), ((1,), (0,)))
    for j in range(nbp):
        both = jnp.concatenate([even[j * half:(j + 1) * half], odd[j * half:(j + 1) * half]], axis=0)
        shape = (bs, 2 * chan)
        lead, live = block_facts(p, j, nb, bs, m_count, shape)
        one = lead.astype(jnp.int32)
        pick = jnp.where(jnp.broadcast_to(one, shape) == 1, both[:, :2 * chan], both[:, 2 * chan:])
        if not first:
            pick = pick + prev_ref[j]
        if last:
            pick = jnp.where(live, pick, 0.0)
        out_ref[j] = pick.astype(out_ref.dtype)


def direct(owners, leg, gauss, got, prev, chunk, dims, last):
    nbp, bs, nb, m_count, rows, stride, chan = dims
    pairs = owners.shape[0]
    lats = got.shape[0]
    blocks = pl.BlockSpec((nbp, bs, 2 * chan), lambda q, o: (q, 0, 0))
    in_specs = [
        pl.BlockSpec((nbp, bs, lats), lambda q, o: (q, 0, chunk)),
        pl.BlockSpec((lats, chan), lambda q, o: (chunk, 0)),
        pl.BlockSpec((lats, rows, 2 * chan), lambda q, o: (0, 0, 0)),
    ]
    args = [owners, leg, gauss, got]
    alias = {}
    if prev is not None:
        in_specs.append(blocks)
        args.append(prev)
        if not last:
            alias = {4: 0}
    return pl.pallas_call(
        functools.partial(direct_kernel, dims, prev is None, last),
        grid_spec=pltpu.PrefetchScalarGridSpec(
            num_scalar_prefetch=1,
            grid=(pairs,),
            in_specs=in_specs,
            out_specs=blocks,
            scratch_shapes=[pltpu.VMEM((2, lats * stride, chan), F32)],
        ),
        out_shape=jax.ShapeDtypeStruct((pairs * nbp, bs, 2 * chan), BF if last else F32),
        input_output_aliases=alias,
        compiler_params=params(48),
        cost_estimate=pl.CostEstimate(flops=4 * 10**9, bytes_accessed=30 * 10**6, transcendentals=0),
        name="direct_legendre",
    )(*args)


def fourier_basis(pair_ids, m_count, nlon):
    wave = jnp.stack([pair_ids, m_count - 1 - pair_ids], axis=1).reshape(m_count, 1)
    longitude = jnp.arange(nlon, dtype=jnp.int32)[None, :]
    angles = (longitude * wave % nlon).astype(F32) * (2.0 * math.pi / nlon)
    scaled = jnp.stack([jnp.cos(angles), -jnp.sin(angles)], axis=1) * (1.0 / math.sqrt(m_count))
    return scaled.astype(BF).reshape(2 * m_count, nlon)


def per_device(spectrum, owners, legendre, gauss_weights):
    pairs = owners.shape[0]
    devices = lax.axis_size("lat")
    blocks, bs, cols = spectrum.shape
    nbp = blocks // pairs
    nb = nbp - 1
    chan = cols // 2
    m_count = 2 * pairs * devices
    nlon = 2 * m_count
    latp = legendre.shape[2]
    here = latp // devices
    chunks = CHUNKS if here % CHUNKS == 0 else 1
    tc = here // chunks
    lats = devices * tc
    rows = 4 * pairs
    stride = -(-rows // 16) * 16
    dims = (nbp, bs, nb, m_count, rows, stride, chan)

    all_owners = lax.all_gather(owners, "lat", axis=0, tiled=True)
    mine = lax.dynamic_slice(all_owners, (lax.axis_index("lat") * pairs,), (pairs,))

    place = jnp.arange(latp, dtype=jnp.int32).reshape(devices, chunks, tc).transpose(1, 0, 2).reshape(latp)
    onehot = (jnp.arange(latp, dtype=jnp.int32)[:, None] == place[None, :]).astype(BF)
    leg = jnp.dot(legendre.reshape(blocks * bs, latp), onehot, preferred_element_type=F32).astype(BF)
    leg = leg.reshape(blocks, bs, latp)
    gauss = gauss_weights.reshape(devices, chunks, tc).transpose(1, 0, 2).reshape(latp, 1)
    gauss = jnp.broadcast_to(gauss, (latp, chan))

    received = []
    for c in range(chunks):
        out = inverse(mine, leg, spectrum, c, lats, dims)
        out = out.reshape(devices, tc, rows, cols)
        received.append(lax.all_to_all(out, "lat", split_axis=0, concat_axis=0, tiled=True))

    turned = fourier_basis(all_owners, m_count, nlon)
    table = turned.T
    grid = None
    tendency = None
    aligned = rows % 16 == 0
    grid_shape = (here, 2, nlon, chan)
    arrived = []
    for c in range(chunks):
        got = received[c]
        if not aligned:
            got = got.transpose(1, 0, 2, 3).reshape(1, tc, devices * rows, cols)
        grid, send = fourier(table, turned, got, grid, c, grid_shape)
        if not aligned:
            send = send.reshape(tc, devices, rows, cols).transpose(1, 0, 2, 3)
        arrived.append(lax.all_to_all(send, "lat", split_axis=0, concat_axis=0, tiled=True))
    for c in range(chunks):
        got = arrived[c].reshape(lats, rows, cols)
        tendency = direct(mine, leg, gauss, got, tendency, c, dims, c == chunks - 1)
    return grid, tendency


def solution(mesh):
    in_specs = (P(("grp", "lat"), None, None), P("lat"), P("lat", None, None), P())
    out_specs = (P(("grp", "lat"), None, None, None), P(("grp", "lat"), None, None))
    return jax.shard_map(
        per_device, mesh=mesh, in_specs=in_specs, out_specs=out_specs, check_vma=False
    )
```

time: 1230 us -> 894 us (0.73)
  blocking collectives: 369 us -> 42 us
  Pallas kernels: 0 us -> 230 us
  local copies, waits for them, and re-layouts: 255 us -> 56.9 us
  waiting for transfers between devices: 328 us -> 460 us
  matrix products: 146 us -> 28.7 us
  other arithmetic: 105 us -> 23.3 us
  starting transfers between devices: 12.1 us -> 40.8 us
    unnamed x1, blocking collectives: 369 us -> 42 us
    pallas_call x0 -> x15, Pallas kernels: none -> 230 us  [the longest x5 81.1 us: direct(): pl.pallas_call(functools.partial(direct_kernel, dims, prev is None, last)...]
    all_to_all x2 -> x10, waiting for transfers between devices: 328 us -> 460 us  [the longest x5 237 us: per_device(): lax.all_to_all(out, 'lat', split_axis=0, concat_axis=0, tiled=True)]
    dot_general x6 -> x1, matrix products: 146 us -> 28.7 us  [per_device(): jnp.dot(legendre.reshape(blocks * bs, latp), onehot, preferred_element_ty...]
    reshape x2, local copies, waits for them, and re-layouts: 36.1 us -> 0.2 us  [the longest x1 0.1 us: per_device(): jnp.arange(latp, dtype=jnp.int32).reshape(devices, chunks, tc)]
    transpose x2, local copies, waits for them, and re-layouts: 40.8 us -> 6.68 us  [the longest x1 6.66 us: per_device(): table = turned.T]
    broadcast_in_dim x5 -> x2, local copies, waits for them, and re-layouts: 30.8 us -> 0.24 us  [per_device(): gauss = jnp.broadcast_to(gauss, (latp, chan))]
    all_to_all x2 -> x10, starting transfers between devices: 12.1 us -> 40.8 us  [the longest x5 20.5 us: per_device(): lax.all_to_all(send, 'lat', split_axis=0, concat_axis=0, tiled=True)]
  transfers between devices with their start and end apart: 2 -> 10, of which waited for: 1 -> 10; matrix products, arithmetic and copies ran while one was open for 6% -> 6% of each run, Pallas kernels for 0% -> 23%
where the time goes in v1:
time: 894 us; the launch traced here: 883 us
  waiting for transfers between devices  460 us (51%)
  Pallas kernels  230 us (26%)
  local copies, waits for them, and re-layouts  56.9 us (6%)
  blocking collectives  42 us (5%)
  starting transfers between devices  40.8 us (5%)
  matrix products  28.7 us (3%)
  other arithmetic  23.3 us (3%)
    all_to_all x5, waiting for transfers between devices, per_device(): lax.all_to_all(out, 'lat', split_axis=0, concat_axis=0, tiled=True)  237 us
    all_to_all x5, waiting for transfers between devices, per_device(): lax.all_to_all(send, 'lat', split_axis=0, concat_axis=0, tiled=True)  224 us
    pallas_call x5, Pallas kernels, direct(): pl.pallas_call(functools.partial(direct_kernel, dims, prev is None, last)...  81.1 us
    pallas_call x5, Pallas kernels, fourier(): pl.pallas_call(kernel, grid=(lats,), in_specs=in_specs, out_specs=[pl.Blo...  80.7 us
    pallas_call x5, Pallas kernels, inverse(): pl.pallas_call(functools.partial(inverse_kernel, dims), grid_spec=pltpu.P...  68 us
    unnamed x1, blocking collectives  42 us
    dot_general x1, matrix products, per_device(): jnp.dot(legendre.reshape(blocks * bs, latp), onehot, preferred_element_ty...  28.7 us
    all_to_all x5, starting transfers between devices, per_device(): lax.all_to_all(send, 'lat', split_axis=0, concat_axis=0, tiled=True)  20.5 us
  transfers between devices with their start and end apart: 10, of which 10 were waited for; matrix products, arithmetic and copies ran while one was open for 6% of the time, Pallas kernels for 23%

profile of v1, /device:TPU:0, one launch (start us, length us, event | category | flops | bytes accessed | tf_op | source)
XLA Modules:
  0.0 882.8 jit_solution(4196659214241056335)
XLA Ops:
  1.5 42.0 %all-reduce = s32[384]{0:T(512)S(1)} all-reduce(s32[384]{0:T(512)S(1)} %dynamic-update-slice), channel_id=1, replica_groups=mesh['grp'=1,'lat'=32] {'lat'}, use_global_device_ids=true, to_apply=%add | all-reduce | flops 384 | bytes 3072
  43.6 28.7 %fusion = bf16[10752,640]{0,1:T(8,128)(2,1)} fusion(bf16[10752,640]{1,0:T(8,128)(2,1)} %bitcast.32, s32[640]{0:T(1024)S(1)} %reshape.202), kind=kOutput, calls=%fused_computation.1 | convolution fusion | flops 8815738880 | bytes 27527680 | tf_op jit(solution)/shard_map/dot_general | solution.py:253
  72.4 18.2 %copy.29 = bf16[10752,640]{1,0:T(8,128)(2,1)} copy(bf16[10752,640]{0,1:T(8,128)(2,1)} %fusion) | data formatting | bytes 27525120 | tf_op jit(solution)/shard_map/convert_element_type | solution.py:253
  90.6 13.6 %inverse_legendre.9 = bf16[128,48,256]{2,1,0:T(8,128)(2,1)} custom-call(s32[12]{0:T(128)S(1)} %dynamic_slice.3.owners_ref, bf16[84,128,640]{2,1,0:T(8,128)(2,1)} %bitcast.20, bf16[84,128,256]{2,1,0:T(8,128)(2,1)} %spec_ref.9), custom_call_target="tpu_custom_call" | custom-call | flops 4000000000 | bytes 15000000 | tf_op jit(solution)/shard_map/inverse_legendre/pallas_call | solution.py:69
  104.2 4.4 all-to-all-start.4
  108.7 13.6 %inverse_legendre.8 = bf16[128,48,256]{2,1,0:T(8,128)(2,1)} custom-call(s32[12]{0:T(128)S(1)} %dynamic_slice.3.owners_ref, bf16[84,128,640]{2,1,0:T(8,128)(2,1)} %bitcast.21, bf16[84,128,256]{2,1,0:T(8,128)(2,1)} %spec_ref.9), custom_call_target="tpu_custom_call" | custom-call | flops 4000000000 | bytes 15000000 | tf_op jit(solution)/shard_map/inverse_legendre/pallas_call | solution.py:69
  122.3 57.9 %all-to-all-done.4.c = bf16[32,4,48,256]{3,2,1,0:T(8,128)(2,1)S(1)} async-done(((bf16[32,4,48,256]{3,2,1,0:T(8,128)(2,1)}), bf16[32,4,48,256]{3,2,1,0:T(8,128)(2,1)S(1)}, u32[]{:S(2)}, u32[]{:S(2)}) %all-to-all-start.4) | async-done | bytes 3145760 | tf_op jit(solution)/shard_map/all_to_all | solution.py:262
  180.1 1.7 copy-done.8
  181.8 3.9 all-to-all-start.3
  185.7 13.6 %inverse_legendre.7 = bf16[128,48,256]{2,1,0:T(8,128)(2,1)} custom-call(s32[12]{0:T(128)S(1)} %dynamic_slice.3.owners_ref, bf16[84,128,640]{2,1,0:T(8,128)(2,1)} %bitcast.22, bf16[84,128,256]{2,1,0:T(8,128)(2,1)} %spec_ref.9), custom_call_target="tpu_custom_call" | custom-call | flops 4000000000 | bytes 15000000 | tf_op jit(solution)/shard_map/inverse_legendre/pallas_call | solution.py:69
  199.3 57.9 %all-to-all-done.3.recv_ref = bf16[32,4,48,256]{3,2,1,0:T(8,128)(2,1)S(1)} async-done(((bf16[32,4,48,256]{3,2,1,0:T(8,128)(2,1)}), bf16[32,4,48,256]{3,2,1,0:T(8,128)(2,1)S(1)}, u32[]{:S(2)}, u32[]{:S(2)}) %all-to-all-start.3) | async-done | bytes 3145760 | tf_op jit(solution)/shard_map/all_to_all | solution.py:262
  257.2 1.7 copy-done.7
  258.9 3.9 all-to-all-start.2
  262.8 13.6 %inverse_legendre.6 = bf16[128,48,256]{2,1,0:T(8,128)(2,1)} custom-call(s32[12]{0:T(128)S(1)} %dynamic_slice.3.owners_ref, bf16[84,128,640]{2,1,0:T(8,128)(2,1)} %bitcast.23, bf16[84,128,256]{2,1,0:T(8,128)(2,1)} %spec_ref.9), custom_call_target="tpu_custom_call" | custom-call | flops 4000000000 | bytes 15000000 | tf_op jit(solution)/shard_map/inverse_legendre/pallas_call | solution.py:69
  276.4 57.9 %all-to-all-done.2.recv_ref = bf16[32,4,48,256]{3,2,1,0:T(8,128)(2,1)S(1)} async-done(((bf16[32,4,48,256]{3,2,1,0:T(8,128)(2,1)}), bf16[32,4,48,256]{3,2,1,0:T(8,128)(2,1)S(1)}, u32[]{:S(2)}, u32[]{:S(2)}) %all-to-all-start.2) | async-done | bytes 3145760 | tf_op jit(solution)/shard_map/all_to_all | solution.py:262
  334.3 1.7 copy-done.6
  336.0 3.9 all-to-all-start.1
  340.0 13.6 %inverse_legendre.5 = bf16[128,48,256]{2,1,0:T(8,128)(2,1)} custom-call(s32[12]{0:T(128)S(1)} %dynamic_slice.3.owners_ref, bf16[84,128,640]{2,1,0:T(8,128)(2,1)} %bitcast.24, bf16[84,128,256]{2,1,0:T(8,128)(2,1)} %spec_ref.9), custom_call_target="tpu_custom_call" | custom-call | flops 4000000000 | bytes 15000000 | tf_op jit(solution)/shard_map/inverse_legendre/pallas_call | solution.py:69
  353.5 57.9 %all-to-all-done.1.recv_ref = bf16[32,4,48,256]{3,2,1,0:T(8,128)(2,1)S(1)} async-done(((bf16[32,4,48,256]{3,2,1,0:T(8,128)(2,1)}), bf16[32,4,48,256]{3,2,1,0:T(8,128)(2,1)S(1)}, u32[]{:S(2)}, u32[]{:S(2)}) %all-to-all-start.1) | async-done | bytes 3145760 | tf_op jit(solution)/shard_map/all_to_all | solution.py:262
  411.4 1.7 copy-done.5
  413.1 4.1 all-to-all-start
  417.6 19.7 %fusion.6 = (f32[768,1,1536]{2,0,1:T(8,128)S(1)}, f32[768,1,1536]{2,0,1:T(8,128)S(1)}) fusion(s32[768]{0:T(1024)S(1)} %mul.55), kind=kLoop, calls=%fused_computation.11 | loop fusion | flops 11796480 | bytes 9440256 | tf_op jit(solution)/shard_map/cos | solution.py:226
  437.2 3.6 fusion.1
  440.8 9.4 %copy.28 = bf16[768,2,1536]{2,1,0:T(2,128)(2,1)} copy(bf16[768,2,1536]{2,0,1:T(8,128)(2,1)} %fusion.1) | data formatting | bytes 9437184 | tf_op jit(solution)/shard_map/convert_element_type | solution.py:227
  450.2 10.7 %convert_element_type.30.b.turned_ref = bf16[1536,1536]{1,0:T(8,128)(2,1)} reshape(bf16[768,2,1536]{2,1,0:T(2,128)(2,1)} %copy.28) | data formatting | bytes 9437184 | tf_op jit(solution)/shard_map/convert_element_type | solution.py:227
  460.9 6.7 copy.34.a.table_ref
  467.5 16.1 %fourier_step.5 = (bf16[20,2,1536,128]{3,2,1,0:T(8,128)(2,1)}, bf16[32,4,48,256]{3,2,1,0:T(8,128)(2,1)}) custom-call(bf16[1536,1536]{1,0:T(8,128)(2,1)} %copy.34.a.table_ref, bf16[1536,1536]{1,0:T(8,128)(2,1)} %convert_element_type.30.b.turned_ref, bf16[32,4,48,256]{3,2,1,0:T(8,128)(2,1)} %copy-done.8), custom_call_target="tpu_custom_call" | custom-call | flops 9663676416 | bytes 20000000 | tf_op jit(solution)/shard_map/fourier_step/pallas_call | solution.py:128
  483.6 5.1 all-to-all-done.recv_ref
  490.3 4.3 all-to-all-start.9
  494.7 16.2 %fourier_step.6 = (bf16[20,2,1536,128]{3,2,1,0:T(8,128)(2,1)}, bf16[32,4,48,256]{3,2,1,0:T(8,128)(2,1)}) custom-call(bf16[1536,1536]{1,0:T(8,128)(2,1)} %copy.34.a.table_ref, bf16[1536,1536]{1,0:T(8,128)(2,1)} %convert_element_type.30.b.turned_ref, bf16[32,4,48,256]{3,2,1,0:T(8,128)(2,1)} %copy-done.7, ...), custom_call_target="tpu_custom_call", output_to_operand_aliasing={{0}: (3, {})} | custom-call | flops 9663676416 | bytes 20000000 | tf_op jit(solution)/shard_map/fourier_step/pallas_call | solution.py:128
  510.8 55.3 %all-to-all-done.9 = bf16[32,4,48,256]{3,2,1,0:T(8,128)(2,1)S(1)} async-done(((bf16[32,4,48,256]{3,2,1,0:T(8,128)(2,1)}), bf16[32,4,48,256]{3,2,1,0:T(8,128)(2,1)S(1)}, u32[]{:S(2)}, u32[]{:S(2)}) %all-to-all-start.9) | async-done | bytes 3145760 | tf_op jit(solution)/shard_map/all_to_all | solution.py:278
  566.1 4.0 all-to-all-start.8
  570.2 16.2 %fourier_step.7 = (bf16[20,2,1536,128]{3,2,1,0:T(8,128)(2,1)}, bf16[32,4,48,256]{3,2,1,0:T(8,128)(2,1)}) custom-call(bf16[1536,1536]{1,0:T(8,128)(2,1)} %copy.34.a.table_ref, bf16[1536,1536]{1,0:T(8,128)(2,1)} %convert_element_type.30.b.turned_ref, bf16[32,4,48,256]{3,2,1,0:T(8,128)(2,1)} %copy-done.6, ...), custom_call_target="tpu_custom_call", output_to_operand_aliasing={{0}: (3, {})} | custom-call | flops 9663676416 | bytes 20000000 | tf_op jit(solution)/shard_map/fourier_step/pallas_call | solution.py:128
  586.3 55.3 %all-to-all-done.8 = bf16[32,4,48,256]{3,2,1,0:T(8,128)(2,1)} async-done(((bf16[32,4,48,256]{3,2,1,0:T(8,128)(2,1)}), bf16[32,4,48,256]{3,2,1,0:T(8,128)(2,1)}, u32[]{:S(2)}, u32[]{:S(2)}) %all-to-all-start.8) | async-done | bytes 3145760 | tf_op jit(solution)/shard_map/all_to_all | solution.py:278
  641.6 3.9 all-to-all-start.7
  645.6 16.2 %fourier_step.8 = (bf16[20,2,1536,128]{3,2,1,0:T(8,128)(2,1)}, bf16[32,4,48,256]{3,2,1,0:T(8,128)(2,1)}) custom-call(bf16[1536,1536]{1,0:T(8,128)(2,1)} %copy.34.a.table_ref, bf16[1536,1536]{1,0:T(8,128)(2,1)} %convert_element_type.30.b.turned_ref, bf16[32,4,48,256]{3,2,1,0:T(8,128)(2,1)} %copy-done.5, ...), custom_call_target="tpu_custom_call", output_to_operand_aliasing={{0}: (3, {})} | custom-call | flops 9663676416 | bytes 20000000 | tf_op jit(solution)/shard_map/fourier_step/pallas_call | solution.py:128
  661.7 55.3 %all-to-all-done.7 = bf16[32,4,48,256]{3,2,1,0:T(8,128)(2,1)S(1)} async-done(((bf16[32,4,48,256]{3,2,1,0:T(8,128)(2,1)}), bf16[32,4,48,256]{3,2,1,0:T(8,128)(2,1)S(1)}, u32[]{:S(2)}, u32[]{:S(2)}) %all-to-all-start.7) | async-done | bytes 3145760 | tf_op jit(solution)/shard_map/all_to_all | solution.py:278
  717.0 4.0 all-to-all-start.6
  721.1 16.1 %fourier_step.9 = (bf16[20,2,1536,128]{3,2,1,0:T(8,128)(2,1)}, bf16[32,4,48,256]{3,2,1,0:T(8,128)(2,1)}) custom-call(bf16[1536,1536]{1,0:T(8,128)(2,1)} %copy.34.a.table_ref, bf16[1536,1536]{1,0:T(8,128)(2,1)} %convert_element_type.30.b.turned_ref, bf16[32,4,48,256]{3,2,1,0:T(8,128)(2,1)} %copy-done.4, ...), custom_call_target="tpu_custom_call", output_to_operand_aliasing={{0}: (3, {})} | custom-call | flops 9663676416 | bytes 20000000 | tf_op jit(solution)/shard_map/fourier_step/pallas_call | solution.py:128
  737.2 55.3 %all-to-all-done.6 = bf16[32,4,48,256]{3,2,1,0:T(8,128)(2,1)} async-done(((bf16[32,4,48,256]{3,2,1,0:T(8,128)(2,1)}), bf16[32,4,48,256]{3,2,1,0:T(8,128)(2,1)}, u32[]{:S(2)}, u32[]{:S(2)}) %all-to-all-start.6) | async-done | bytes 3145760 | tf_op jit(solution)/shard_map/all_to_all | solution.py:278
  792.5 4.1 all-to-all-start.5
  797.0 1.9 copy-done.1
  798.9 13.3 %direct_legendre.5.rest_0_ = f32[84,128,256]{2,1,0:T(8,128)} custom-call(s32[12]{0:T(128)S(1)} %dynamic_slice.3.owners_ref, bf16[84,128,640]{2,1,0:T(8,128)(2,1)} %bitcast.25, f32[640,128]{1,0:T(8,128)S(1)} %broadcast_in_dim.10.gauss_ref, bf16[128,48,256]{2,1,0:T(8,128)(2,1)S(1)} %bitcast.18), custom_call_target="tpu_custom_call" | custom-call | flops 4000000000 | bytes 30000000 | tf_op jit(solution)/shard_map/direct_legendre/pallas_call | solution.py:205
  812.2 18.3 %direct_legendre.6.rest_0_ = f32[84,128,256]{2,1,0:T(8,128)} custom-call(s32[12]{0:T(128)S(1)} %dynamic_slice.3.owners_ref, bf16[84,128,640]{2,1,0:T(8,128)(2,1)} %bitcast.26, f32[640,128]{1,0:T(8,128)S(1)} %broadcast_in_dim.10.gauss_ref, bf16[128,48,256]{2,1,0:T(8,128)(2,1)} %bitcast.13.got_ref, ...), custom_call_target="tpu_custom_call", output_to_operand_aliasing={{}: (4, {})} | custom-call | flops 4000000000 | bytes 30000000 | tf_op jit(solution)/shard_map/direct_legendre/pallas_call | solution.py:205
  830.5 17.0 %direct_legendre.7.rest_0_ = f32[84,128,256]{2,1,0:T(8,128)} custom-call(s32[12]{0:T(128)S(1)} %dynamic_slice.3.owners_ref, bf16[84,128,640]{2,1,0:T(8,128)(2,1)} %bitcast.27, f32[640,128]{1,0:T(8,128)S(1)} %broadcast_in_dim.10.gauss_ref, bf16[128,48,256]{2,1,0:T(8,128)(2,1)S(1)} %bitcast.19, ...), custom_call_target="tpu_custom_call", output_to_operand_aliasing={{}: (4, {})} | custom-call | flops 4000000000 | bytes 30000000 | tf_op jit(solution)/shard_map/direct_legendre/pallas_call | solution.py:205
  847.5 18.0 %direct_legendre.8.rest_0_ = f32[84,128,256]{2,1,0:T(8,128)} custom-call(s32[12]{0:T(128)S(1)} %dynamic_slice.3.owners_ref, bf16[84,128,640]{2,1,0:T(8,128)(2,1)} %bitcast.28, f32[640,128]{1,0:T(8,128)S(1)} %broadcast_in_dim.10.gauss_ref, bf16[128,48,256]{2,1,0:T(8,128)(2,1)} %bitcast.11.got_ref, ...), custom_call_target="tpu_custom_call", output_to_operand_aliasing={{}: (4, {})} | custom-call | flops 4000000000 | bytes 30000000 | tf_op jit(solution)/shard_map/direct_legendre/pallas_call | solution.py:205
  865.5 2.6 all-to-all-done.5
  868.1 14.6 %direct_legendre.9 = bf16[84,128,256]{2,1,0:T(8,128)(2,1)} custom-call(s32[12]{0:T(128)S(1)} %dynamic_slice.3.owners_ref, bf16[84,128,640]{2,1,0:T(8,128)(2,1)} %bitcast.29, f32[640,128]{1,0:T(8,128)S(1)} %broadcast_in_dim.10.gauss_ref, bf16[128,48,256]{2,1,0:T(8,128)(2,1)S(1)} %bitcast.17, f32[84,128,256]{2,1,0:T(8,128)} %direct_legendre.8.rest_0_), custom_call_target="tpu_custom_call" | custom-call | flops 4000000000 | bytes 30000000 | tf_op jit(solution)/shard_map/direct_legendre/pallas_call | solution.py:205
  (30 shorter events, 3.4 us)
Async XLA Ops:
  104.2 75.9 %all-to-all-start.4 = ((bf16[32,4,48,256]{3,2,1,0:T(8,128)(2,1)}), bf16[32,4,48,256]{3,2,1,0:T(8,128)(2,1)S(1)}, u32[]{:S(2)}, u32[]{:S(2)}) async-start(bf16[32,4,48,256]{3,2,1,0:T(8,128)(2,1)} %bitcast.8), calls=%async_computation.4 | async-start | bytes 6291456 | tf_op jit(solution)/shard_map/all_to_all | solution.py:262
  180.1 1.7 copy-start.8
  181.8 75.4 %all-to-all-start.3 = ((bf16[32,4,48,256]{3,2,1,0:T(8,128)(2,1)}), bf16[32,4,48,256]{3,2,1,0:T(8,128)(2,1)S(1)}, u32[]{:S(2)}, u32[]{:S(2)}) async-start(bf16[32,4,48,256]{3,2,1,0:T(8,128)(2,1)} %bitcast.7), calls=%async_computation.3 | async-start | bytes 6291456 | tf_op jit(solution)/shard_map/all_to_all | solution.py:262
  257.2 1.7 copy-start.7
  258.9 75.4 %all-to-all-start.2 = ((bf16[32,4,48,256]{3,2,1,0:T(8,128)(2,1)}), bf16[32,4,48,256]{3,2,1,0:T(8,128)(2,1)S(1)}, u32[]{:S(2)}, u32[]{:S(2)}) async-start(bf16[32,4,48,256]{3,2,1,0:T(8,128)(2,1)} %bitcast.6), calls=%async_computation.2 | async-start | bytes 6291456 | tf_op jit(solution)/shard_map/all_to_all | solution.py:262
  334.3 1.7 copy-start.6
  336.0 75.4 %all-to-all-start.1 = ((bf16[32,4,48,256]{3,2,1,0:T(8,128)(2,1)}), bf16[32,4,48,256]{3,2,1,0:T(8,128)(2,1)S(1)}, u32[]{:S(2)}, u32[]{:S(2)}) async-start(bf16[32,4,48,256]{3,2,1,0:T(8,128)(2,1)} %bitcast.5), calls=%async_computation.1 | async-start | bytes 6291456 | tf_op jit(solution)/shard_map/all_to_all | solution.py:262
  411.4 1.7 copy-start.5
  413.1 75.6 %all-to-all-start = ((bf16[32,4,48,256]{3,2,1,0:T(8,128)(2,1)}), bf16[32,4,48,256]{3,2,1,0:T(8,128)(2,1)S(1)}, u32[]{:S(2)}, u32[]{:S(2)}) async-start(bf16[32,4,48,256]{3,2,1,0:T(8,128)(2,1)} %bitcast.4), calls=%async_computation | async-start | bytes 6291456 | tf_op jit(solution)/shard_map/all_to_all | solution.py:262
  488.7 1.7 copy-start.4
  490.3 75.8 %all-to-all-start.9 = ((bf16[32,4,48,256]{3,2,1,0:T(8,128)(2,1)}), bf16[32,4,48,256]{3,2,1,0:T(8,128)(2,1)S(1)}, u32[]{:S(2)}, u32[]{:S(2)}) async-start(bf16[32,4,48,256]{3,2,1,0:T(8,128)(2,1)} %get-tuple-element.21), calls=%async_computation.9 | async-start | bytes 6291456 | tf_op jit(solution)/shard_map/all_to_all | solution.py:278
  566.1 20.2 %copy-start = (bf16[32,4,48,256]{3,2,1,0:T(8,128)(2,1)}, bf16[32,4,48,256]{3,2,1,0:T(8,128)(2,1)S(1)}, u32[]{:S(2)}) copy-start(bf16[32,4,48,256]{3,2,1,0:T(8,128)(2,1)S(1)} %all-to-all-done.9) | copy-start | bytes 9437188
  566.1 75.5 %all-to-all-start.8 = ((bf16[32,4,48,256]{3,2,1,0:T(8,128)(2,1)}), bf16[32,4,48,256]{3,2,1,0:T(8,128)(2,1)}, u32[]{:S(2)}, u32[]{:S(2)}) async-start(bf16[32,4,48,256]{3,2,1,0:T(8,128)(2,1)} %get-tuple-element.20), calls=%async_computation.8 | async-start | bytes 6291456 | tf_op jit(solution)/shard_map/all_to_all | solution.py:278
  641.6 75.4 %all-to-all-start.7 = ((bf16[32,4,48,256]{3,2,1,0:T(8,128)(2,1)}), bf16[32,4,48,256]{3,2,1,0:T(8,128)(2,1)S(1)}, u32[]{:S(2)}, u32[]{:S(2)}) async-start(bf16[32,4,48,256]{3,2,1,0:T(8,128)(2,1)} %get-tuple-element.19), calls=%async_computation.7 | async-start | bytes 6291456 | tf_op jit(solution)/shard_map/all_to_all | solution.py:278
  717.0 20.2 %copy-start.2 = (bf16[32,4,48,256]{3,2,1,0:T(8,128)(2,1)}, bf16[32,4,48,256]{3,2,1,0:T(8,128)(2,1)S(1)}, u32[]{:S(2)}) copy-start(bf16[32,4,48,256]{3,2,1,0:T(8,128)(2,1)S(1)} %all-to-all-done.7) | copy-start | bytes 9437188
  717.0 75.5 %all-to-all-start.6 = ((bf16[32,4,48,256]{3,2,1,0:T(8,128)(2,1)}), bf16[32,4,48,256]{3,2,1,0:T(8,128)(2,1)}, u32[]{:S(2)}, u32[]{:S(2)}) async-start(bf16[32,4,48,256]{3,2,1,0:T(8,128)(2,1)} %get-tuple-element.18), calls=%async_computation.6 | async-start | bytes 6291456 | tf_op jit(solution)/shard_map/all_to_all | solution.py:278
  737.2 59.4 %copy-start.9 = (f32[640]{0:T(1024)S(1)}, f32[640]{0:T(1024)}, u32[]{:S(2)}) copy-start(f32[640]{0:T(1024)} %param.7) | copy-start | bytes 7684
  792.5 75.6 %all-to-all-start.5 = ((bf16[32,4,48,256]{3,2,1,0:T(8,128)(2,1)}), bf16[32,4,48,256]{3,2,1,0:T(8,128)(2,1)S(1)}, u32[]{:S(2)}, u32[]{:S(2)}) async-start(bf16[32,4,48,256]{3,2,1,0:T(8,128)(2,1)} %get-tuple-element.17), calls=%async_computation.5 | async-start | bytes 6291456 | tf_op jit(solution)/shard_map/all_to_all | solution.py:278
  797.0 1.9 copy-start.1
  812.2 18.3 %copy-start.3 = (bf16[32,4,48,256]{3,2,1,0:T(8,128)(2,1)S(1)}, bf16[32,4,48,256]{3,2,1,0:T(8,128)(2,1)}, u32[]{:S(2)}) copy-start(bf16[32,4,48,256]{3,2,1,0:T(8,128)(2,1)} %copy-done.2) | copy-start | bytes 9437188

commit v2 on v1

--- a/solution.py
+++ b/solution.py
@@ -10,7 +10,6 @@
 
 BF = jnp.bfloat16
 F32 = jnp.float32
-CHUNKS = 5
 
 
 def dot(a, b, dims):
@@ -33,7 +32,7 @@
     return lead, degree >= m
 
 
-def inverse_kernel(dims, owners_ref, leg_ref, spec_ref, out_ref, acc_ref):
+def inverse_kernel(dims, owners_ref, leg_ref, spec_ref, order_ref, out_ref, table_ref, acc_ref):
     nbp, bs, nb, m_count, rows, stride, chan = dims
     q = pl.program_id(0)
     half = bs // 2
@@ -47,8 +46,10 @@
         both = jnp.concatenate([s * one, s * (1.0 - one)], axis=1).astype(BF)
         firsts.append(both[:half])
         seconds.append(both[half:])
-    te = jnp.concatenate([leg_ref[j, :half] for j in range(nbp)], axis=0)
-    to = jnp.concatenate([leg_ref[j, half:] for j in range(nbp)], axis=0)
+    picked = dot(leg_ref[...].reshape(nbp * bs, leg_ref.shape[2]), order_ref[...], ((1,), (0,))).astype(BF)
+    table_ref[...] = picked.reshape(table_ref.shape)
+    te = jnp.concatenate([picked[j * bs:j * bs + half] for j in range(nbp)], axis=0)
+    to = jnp.concatenate([picked[j * bs + half:(j + 1) * bs] for j in range(nbp)], axis=0)
     sym = dot(te, jnp.concatenate(firsts, axis=0), ((0,), (0,)))
     anti = dot(to, jnp.concatenate(seconds, axis=0), ((0,), (0,)))
     lats = sym.shape[0]
@@ -58,31 +59,45 @@
 
     @pl.when(q == pl.num_programs(0) - 1)
     def _():
-        for h in range(2):
-            full = acc_ref[h].reshape(lats, stride, chan)
-            out_ref[:, :, h * chan:(h + 1) * chan] = full[:, :rows].astype(BF)
-
-
-def inverse(owners, leg, spec, chunk, lats, dims):
+        def move(i, _):
+            for h in range(2):
+                full = acc_ref[h, pl.ds(i * 16 * stride, 16 * stride), :].reshape(16, stride, chan)
+                out_ref[pl.ds(i * 16, 16), :, h * chan:(h + 1) * chan] = full[:, :rows].astype(BF)
+            return 0
+
+        lax.fori_loop(0, lats // 16, move, 0)
+
+
+def inverse(owners, leg, spec, order, dims):
     nbp, bs, nb, m_count, rows, stride, chan = dims
     pairs = owners.shape[0]
+    latp, lats = order.shape
     return pl.pallas_call(
         functools.partial(inverse_kernel, dims),
         grid_spec=pltpu.PrefetchScalarGridSpec(
             num_scalar_prefetch=1,
             grid=(pairs,),
             in_specs=[
-                pl.BlockSpec((nbp, bs, lats), lambda q, o: (q, 0, chunk)),
+                pl.BlockSpec((nbp, bs, latp), lambda q, o: (q, 0, 0)),
                 pl.BlockSpec((nbp, bs, 2 * chan), lambda q, o: (q, 0, 0)),
+                pl.BlockSpec((latp, lats), lambda q, o: (0, 0)),
             ],
-            out_specs=pl.BlockSpec((lats, rows, 2 * chan), lambda q, o: (0, 0, 0)),
+            out_specs=[
+                pl.BlockSpec((lats, rows, 2 * chan), lambda q, o: (0, 0, 0)),
+                pl.BlockSpec((nbp, bs, lats), lambda q, o: (q, 0, 0)),
+            ],
             scratch_shapes=[pltpu.VMEM((2, lats * stride, chan), F32)],
         ),
-        out_shape=jax.ShapeDtypeStruct((lats, rows, 2 * chan), BF),
-        compiler_params=params(48),
-        cost_estimate=pl.CostEstimate(flops=4 * 10**9, bytes_accessed=15 * 10**6, transcendentals=0),
+        out_shape=[
+            jax.ShapeDtypeStruct((lats, rows, 2 * chan), BF),
+            jax.ShapeDtypeStruct((pairs * nbp, bs, lats), BF),
+        ],
+        compiler_params=params(58),
+        cost_estimate=pl.CostEstimate(
+            flops=lats * 90 * 10**6, bytes_accessed=20 * 10**6 + lats * 10**5, transcendentals=0
+        ),
         name="inverse_legendre",
-    )(owners, leg, spec)
+    )(owners, leg, spec, order)
 
 
 def fourier_kernel(chan, table_ref, turned_ref, recv_ref, prev_ref, grid_ref, send_ref):
@@ -107,7 +122,7 @@
     send_ref[:, 0] = coeffs.reshape(groups, rows, cols)
 
 
-def fourier(table, turned, recv, prev, chunk, grid_shape):
+def fourier(table, turned, recv, prev, start, grid_shape):
     groups, lats, rows, cols = recv.shape
     nlon, total = table.shape
     chan = cols // 2
@@ -130,7 +145,7 @@
         grid=(lats,),
         in_specs=in_specs,
         out_specs=[
-            pl.BlockSpec((1, 2, nlon, chan), lambda t: (chunk * lats + t, 0, 0, 0)),
+            pl.BlockSpec((1, 2, nlon, chan), lambda t: (start + t, 0, 0, 0)),
             part,
         ],
         out_shape=[
@@ -155,11 +170,15 @@
 
     @pl.when(q == 0)
     def _():
-        for h in range(2):
-            full = got_ref[:, :, h * chan:(h + 1) * chan].astype(F32)
-            if stride != rows:
-                full = jnp.concatenate([full, jnp.zeros((lats, stride - rows, chan), F32)], axis=1)
-            acc_ref[h] = full.reshape(lats * stride, chan)
+        def move(i, _):
+            for h in range(2):
+                full = got_ref[pl.ds(i * 16, 16), :, h * chan:(h + 1) * chan].astype(F32)
+                if stride != rows:
+                    full = jnp.concatenate([full, jnp.zeros((16, stride - rows, chan), F32)], axis=1)
+                acc_ref[h, pl.ds(i * 16 * stride, 16 * stride), :] = full.reshape(16 * stride, chan)
+            return 0
+
+        lax.fori_loop(0, lats // 16, move, 0)
 
     g = gauss_ref[...]
     syms, antis = [], []
@@ -185,14 +204,14 @@
         out_ref[j] = pick.astype(out_ref.dtype)
 
 
-def direct(owners, leg, gauss, got, prev, chunk, dims, last):
+def direct(owners, leg, gauss, got, prev, dims, last):
     nbp, bs, nb, m_count, rows, stride, chan = dims
     pairs = owners.shape[0]
     lats = got.shape[0]
     blocks = pl.BlockSpec((nbp, bs, 2 * chan), lambda q, o: (q, 0, 0))
     in_specs = [
-        pl.BlockSpec((nbp, bs, lats), lambda q, o: (q, 0, chunk)),
-        pl.BlockSpec((lats, chan), lambda q, o: (chunk, 0)),
+        pl.BlockSpec((nbp, bs, lats), lambda q, o: (q, 0, 0)),
+        pl.BlockSpec((lats, chan), lambda q, o: (0, 0)),
         pl.BlockSpec((lats, rows, 2 * chan), lambda q, o: (0, 0, 0)),
     ]
     args = [owners, leg, gauss, got]
@@ -213,8 +232,10 @@
         ),
         out_shape=jax.ShapeDtypeStruct((pairs * nbp, bs, 2 * chan), BF if last else F32),
         input_output_aliases=alias,
-        compiler_params=params(48),
-        cost_estimate=pl.CostEstimate(flops=4 * 10**9, bytes_accessed=30 * 10**6, transcendentals=0),
+        compiler_params=params(58),
+        cost_estimate=pl.CostEstimate(
+            flops=lats * 40 * 10**6, bytes_accessed=25 * 10**6 + lats * 10**5, transcendentals=0
+        ),
         name="direct_legendre",
     )(*args)
 
@@ -238,47 +259,64 @@
     nlon = 2 * m_count
     latp = legendre.shape[2]
     here = latp // devices
-    chunks = CHUNKS if here % CHUNKS == 0 else 1
-    tc = here // chunks
-    lats = devices * tc
+    fifth = here // 5
+    sizes = (fifth, 3 * fifth, fifth) if here % 5 == 0 else (here,)
+    starts = [sum(sizes[:c]) for c in range(len(sizes))]
     rows = 4 * pairs
     stride = -(-rows // 16) * 16
     dims = (nbp, bs, nb, m_count, rows, stride, chan)
-
-    all_owners = lax.all_gather(owners, "lat", axis=0, tiled=True)
-    mine = lax.dynamic_slice(all_owners, (lax.axis_index("lat") * pairs,), (pairs,))
-
-    place = jnp.arange(latp, dtype=jnp.int32).reshape(devices, chunks, tc).transpose(1, 0, 2).reshape(latp)
-    onehot = (jnp.arange(latp, dtype=jnp.int32)[:, None] == place[None, :]).astype(BF)
-    leg = jnp.dot(legendre.reshape(blocks * bs, latp), onehot, preferred_element_type=F32).astype(BF)
-    leg = leg.reshape(blocks, bs, latp)
-    gauss = gauss_weights.reshape(devices, chunks, tc).transpose(1, 0, 2).reshape(latp, 1)
-    gauss = jnp.broadcast_to(gauss, (latp, chan))
-
-    received = []
-    for c in range(chunks):
-        out = inverse(mine, leg, spectrum, c, lats, dims)
-        out = out.reshape(devices, tc, rows, cols)
-        received.append(lax.all_to_all(out, "lat", split_axis=0, concat_axis=0, tiled=True))
-
+    aligned = rows % 16 == 0
+    grid_shape = (here, 2, nlon, chan)
+
+    copies = jnp.broadcast_to(owners[None, :], (devices, pairs))
+    all_owners = lax.all_to_all(copies, "lat", split_axis=0, concat_axis=0, tiled=True).reshape(-1)
+
+    def swap(x):
+        return lax.all_to_all(x, "lat", split_axis=0, concat_axis=0, tiled=True)
+
+    def places(c):
+        device = jnp.arange(devices, dtype=jnp.int32)[:, None]
+        return (device * here + starts[c] + jnp.arange(sizes[c], dtype=jnp.int32)[None, :]).reshape(-1)
+
+    def inverse_chunk(c):
+        order = (jnp.arange(latp, dtype=jnp.int32)[:, None] == places(c)[None, :]).astype(BF)
+        out, leg = inverse(owners, legendre, spectrum, order, dims)
+        return out.reshape(devices, sizes[c], rows, cols), leg
+
+    def fourier_chunk(c, got, grid):
+        if not aligned:
+            got = got.transpose(1, 0, 2, 3).reshape(1, sizes[c], devices * rows, cols)
+        grid, send = fourier(table, turned, got, grid, starts[c], grid_shape)
+        if not aligned:
+            send = send.reshape(sizes[c], devices, rows, cols).transpose(1, 0, 2, 3)
+        return grid, send
+
+    count = len(sizes)
+    outs, legs = zip(*[inverse_chunk(c) for c in range(count)])
+    outs = list(outs)
+    outs[0], all_owners = lax.optimization_barrier((outs[0], all_owners))
+    received = [swap(outs[0])]
     turned = fourier_basis(all_owners, m_count, nlon)
     table = turned.T
-    grid = None
+    grid, send = fourier_chunk(0, received[0], None)
+    sends = [send]
+    for c in range(1, count):
+        if c == 2:
+            outs[c], sends[0], grid = lax.optimization_barrier((outs[c], sends[0], grid))
+        received.append(swap(outs[c]))
+        if c == 1:
+            sends[0], received[1] = lax.optimization_barrier((sends[0], received[1]))
+    for c in range(1, count):
+        grid, send = fourier_chunk(c, received[c], grid)
+        sends.append(send)
     tendency = None
-    aligned = rows % 16 == 0
-    grid_shape = (here, 2, nlon, chan)
-    arrived = []
-    for c in range(chunks):
-        got = received[c]
-        if not aligned:
-            got = got.transpose(1, 0, 2, 3).reshape(1, tc, devices * rows, cols)
-        grid, send = fourier(table, turned, got, grid, c, grid_shape)
-        if not aligned:
-            send = send.reshape(tc, devices, rows, cols).transpose(1, 0, 2, 3)
-        arrived.append(lax.all_to_all(send, "lat", split_axis=0, concat_axis=0, tiled=True))
-    for c in range(chunks):
-        got = arrived[c].reshape(lats, rows, cols)
-        tendency = direct(mine, leg, gauss, got, tendency, c, dims, c == chunks - 1)
+    for c in range(count):
+        got = swap(sends[c]).reshape(devices * sizes[c], rows, cols)
+        gauss = jnp.broadcast_to(
+            gauss_weights.reshape(devices, here)[:, starts[c]:starts[c] + sizes[c]].reshape(-1, 1),
+            (devices * sizes[c], chan),
+        )
+        tendency = direct(owners, legs[c], gauss, got, tendency, dims, c == count - 1)
     return grid, tendency
 
 

time: 894 us -> 782 us (0.87)
  waiting for transfers between devices: 460 us -> 419 us
  Pallas kernels: 230 us -> 194 us
  blocking collectives: 42 us -> 74.7 us
  matrix products: 28.7 us -> 0 us
  local copies, waits for them, and re-layouts: 56.9 us -> 36.2 us
  starting transfers between devices: 40.8 us -> 27.9 us
    all_to_all x0 -> x1, blocking collectives: none -> 74.7 us  [swap(): return lax.all_to_all(x, 'lat', split_axis=0, concat_axis=0, tiled=True)]
    unnamed x1 -> x0, blocking collectives: 42 us -> none
    all_to_all x10 -> x6, waiting for transfers between devices: 460 us -> 419 us  [the longest x5 419 us: swap(): return lax.all_to_all(x, 'lat', split_axis=0, concat_axis=0, tiled=True)]
    dot_general x1 -> x0, matrix products: 28.7 us -> none  [per_device(): jnp.dot(legendre.reshape(blocks * bs, latp), onehot, preferred_element_ty...]
    pallas_call x5 -> x3, Pallas kernels: 81.1 us -> 54.1 us  [direct(): pl.pallas_call(functools.partial(direct_kernel, dims, prev is None, last)...]
    convert_element_type x1 -> x0, local copies, waits for them, and re-layouts: 18.2 us -> none  [per_device(): jnp.dot(legendre.reshape(blocks * bs, latp), onehot, preferred_element_ty...]
    all_to_all x10 -> x6, starting transfers between devices: 40.8 us -> 27.9 us  [the longest x5 20.6 us: swap(): return lax.all_to_all(x, 'lat', split_axis=0, concat_axis=0, tiled=True)]
    pallas_call x5 -> x3, Pallas kernels: 80.7 us -> 70.8 us  [fourier(): pl.pallas_call(kernel, grid=(lats,), in_specs=in_specs, out_specs=[pl.Blo...]
  transfers between devices with their start and end apart: 10 -> 6, of which waited for: 10 -> 5; matrix products, arithmetic and copies ran while one was open for 6% -> 7% of each run, Pallas kernels for 23% -> 23%
where the time goes in v2:
time: 782 us; the launch traced here: 780 us
  waiting for transfers between devices  419 us (54%)
  Pallas kernels  194 us (25%)
  blocking collectives  74.7 us (10%)
  local copies, waits for them, and re-layouts  36.2 us (5%)
  starting transfers between devices  27.9 us (4%)
  other arithmetic  26.6 us (3%)
    all_to_all x5, waiting for transfers between devices, swap(): return lax.all_to_all(x, 'lat', split_axis=0, concat_axis=0, tiled=True)  419 us
    all_to_all x1, blocking collectives, swap(): return lax.all_to_all(x, 'lat', split_axis=0, concat_axis=0, tiled=True)  74.7 us
    pallas_call x3, Pallas kernels, fourier(): pl.pallas_call(kernel, grid=(lats,), in_specs=in_specs, out_specs=[pl.Blo...  70.8 us
    pallas_call x3, Pallas kernels, inverse(): pl.pallas_call(functools.partial(inverse_kernel, dims), grid_spec=pltpu.P...  69.2 us
    pallas_call x3, Pallas kernels, direct(): pl.pallas_call(functools.partial(direct_kernel, dims, prev is None, last)...  54.1 us
    all_to_all x5, starting transfers between devices, swap(): return lax.all_to_all(x, 'lat', split_axis=0, concat_axis=0, tiled=True)  20.6 us
    convert_element_type x2, local copies, waits for them, and re-layouts, fourier_basis(): return scaled.astype(BF).reshape(2 * m_count, nlon)  20 us
    cos x1, other arithmetic, fourier_basis(): jnp.cos(angles)  19.7 us
  transfers between devices with their start and end apart: 6, of which 5 were waited for; matrix products, arithmetic and copies ran while one was open for 7% of the time, Pallas kernels for 23%

profile of v2, /device:TPU:0, one launch (start us, length us, event | category | flops | bytes accessed | tf_op | source)
XLA Modules:
  0.0 779.8 jit_solution(13829908480332352181)
XLA Ops:
  0.6 1.3 broadcast_in_dim.14
  1.9 7.3 all-to-all-start
  9.3 0.1 add.102
  9.4 0.7 fusion.8.order_ref
  10.1 19.9 %inverse_legendre.3 = (bf16[128,48,256]{2,1,0:T(8,128)(2,1)}, bf16[84,128,128]{2,1,0:T(8,128)(2,1)}) custom-call(s32[12]{0:T(128)} %owners_ref.11, bf16[84,128,640]{2,1,0:T(8,128)(2,1)} %leg_ref.5, bf16[84,128,256]{2,1,0:T(8,128)(2,1)} %spec_ref.5, bf16[640,128]{1,0:T(8,128)(2,1)} %fusion.8.order_ref), custom_call_target="tpu_custom_call" | custom-call | flops 11520000000 | bytes 32800000 | tf_op jit(solution)/shard_map/inverse_legendre/pallas_call | solution.py:75
  30.0 0.5 broadcast.139
  30.5 0.7 reduce.3
  31.2 0.1 reshape.205
  31.3 5.8 all-to-all-start.1
  37.2 0.1 add.115
  37.3 0.9 fusion.7.order_ref
  38.3 29.5 %inverse_legendre.5 = (bf16[384,48,256]{2,1,0:T(8,128)(2,1)}, bf16[84,128,384]{2,1,0:T(8,128)(2,1)}) custom-call(s32[12]{0:T(128)} %owners_ref.11, bf16[84,128,640]{2,1,0:T(8,128)(2,1)} %leg_ref.5, bf16[84,128,256]{2,1,0:T(8,128)(2,1)} %spec_ref.5, bf16[640,384]{1,0:T(8,128)(2,1)} %fusion.7.order_ref), custom_call_target="tpu_custom_call" | custom-call | flops 34560000000 | bytes 58400000 | tf_op jit(solution)/shard_map/inverse_legendre/pallas_call | solution.py:75
  67.7 40.9 %all-to-all-done.1.c = bf16[32,4,48,256]{3,2,1,0:T(8,128)(2,1)S(1)} async-done(((bf16[32,4,48,256]{3,2,1,0:T(8,128)(2,1)}), bf16[32,4,48,256]{3,2,1,0:T(8,128)(2,1)S(1)}, u32[]{:S(2)}, u32[]{:S(2)}) %all-to-all-start.1) | async-done | bytes 3145760 | tf_op jit(solution)/shard_map/all_to_all | solution.py:275
  108.6 1.6 copy-done.1
  110.2 4.2 all-to-all-start.2
  114.6 0.1 add.109
  114.7 0.7 fusion.9.order_ref
  115.4 19.9 %inverse_legendre.4 = (bf16[128,48,256]{2,1,0:T(8,128)(2,1)}, bf16[84,128,128]{2,1,0:T(8,128)(2,1)}) custom-call(s32[12]{0:T(128)} %owners_ref.11, bf16[84,128,640]{2,1,0:T(8,128)(2,1)} %leg_ref.5, bf16[84,128,256]{2,1,0:T(8,128)(2,1)} %spec_ref.5, bf16[640,128]{1,0:T(8,128)(2,1)} %fusion.9.order_ref), custom_call_target="tpu_custom_call" | custom-call | flops 11520000000 | bytes 32800000 | tf_op jit(solution)/shard_map/inverse_legendre/pallas_call | solution.py:75
  135.3 0.1 copy.20
  135.4 0.1 mul.73
  135.6 19.7 %fusion.5 = (f32[768,1,1536]{2,0,1:T(8,128)S(1)}, f32[768,1,1536]{2,0,1:T(8,128)S(1)}) fusion(s32[768]{0:T(1024)S(1)} %mul.73), kind=kLoop, calls=%fused_computation.9 | loop fusion | flops 11796480 | bytes 9440256 | tf_op jit(solution)/shard_map/cos | solution.py:247
  155.3 3.6 fusion
  158.9 9.4 %copy.21 = bf16[768,2,1536]{2,1,0:T(2,128)(2,1)} copy(bf16[768,2,1536]{2,0,1:T(8,128)(2,1)} %fusion) | data formatting | bytes 9437184 | tf_op jit(solution)/shard_map/convert_element_type | solution.py:248
  168.2 10.7 %convert_element_type.33.b.turned_ref = bf16[1536,1536]{1,0:T(8,128)(2,1)} reshape(bf16[768,2,1536]{2,1,0:T(2,128)(2,1)} %copy.21) | data formatting | bytes 9437184 | tf_op jit(solution)/shard_map/convert_element_type | solution.py:248
  178.9 6.6 copy.24.a.table_ref
  185.5 16.1 %fourier_step.3 = (bf16[20,2,1536,128]{3,2,1,0:T(8,128)(2,1)}, bf16[32,4,48,256]{3,2,1,0:T(8,128)(2,1)}) custom-call(bf16[1536,1536]{1,0:T(8,128)(2,1)} %copy.24.a.table_ref, bf16[1536,1536]{1,0:T(8,128)(2,1)} %convert_element_type.33.b.turned_ref, bf16[32,4,48,256]{3,2,1,0:T(8,128)(2,1)} %copy-done.1), custom_call_target="tpu_custom_call" | custom-call | flops 9663676416 | bytes 20000000 | tf_op jit(solution)/shard_map/fourier_step/pallas_call | solution.py:143
  201.6 121.9 %all-to-all-done.2.recv_ref = bf16[32,12,48,256]{3,2,1,0:T(8,128)(2,1)} async-done(((bf16[32,12,48,256]{3,2,1,0:T(8,128)(2,1)}), bf16[32,12,48,256]{3,2,1,0:T(8,128)(2,1)}, u32[]{:S(2)}, u32[]{:S(2)}) %all-to-all-start.2) | async-done | bytes 9437216 | tf_op jit(solution)/shard_map/all_to_all | solution.py:275
  323.5 74.7 %all_to_all.36 = bf16[32,4,48,256]{3,2,1,0:T(8,128)(2,1)} all-to-all(bf16[32,4,48,256]{3,2,1,0:T(8,128)(2,1)} %get-tuple-element.39), channel_id=1, replica_groups=mesh['grp'=1,'lat'=32] {'lat'}, dimensions={0} | all-to-all | bytes 6291456 | tf_op jit(solution)/shard_map/all_to_all | solution.py:275
  398.2 3.8 all-to-all-start.3
  402.1 38.6 %fourier_step.4 = (bf16[20,2,1536,128]{3,2,1,0:T(8,128)(2,1)}, bf16[32,12,48,256]{3,2,1,0:T(8,128)(2,1)}) custom-call(bf16[1536,1536]{1,0:T(8,128)(2,1)} %copy.24.a.table_ref, bf16[1536,1536]{1,0:T(8,128)(2,1)} %convert_element_type.33.b.turned_ref, bf16[32,12,48,256]{3,2,1,0:T(8,128)(2,1)} %all-to-all-done.2.recv_ref, ...), custom_call_target="tpu_custom_call", output_to_operand_aliasing={{0}: (3, {})} | custom-call | flops 28991029248 | bytes 20000000 | tf_op jit(solution)/shard_map/fourier_step/pallas_call | solution.py:143
  440.7 32.7 %all-to-all-done.3.recv_ref = bf16[32,4,48,256]{3,2,1,0:T(8,128)(2,1)S(1)} async-done(((bf16[32,4,48,256]{3,2,1,0:T(8,128)(2,1)}), bf16[32,4,48,256]{3,2,1,0:T(8,128)(2,1)S(1)}, u32[]{:S(2)}, u32[]{:S(2)}) %all-to-all-start.3) | async-done | bytes 3145760 | tf_op jit(solution)/shard_map/all_to_all | solution.py:275
  473.4 1.6 copy-done.2
  475.0 3.9 all-to-all-start.5
  479.0 16.1 %fourier_step.5 = (bf16[20,2,1536,128]{3,2,1,0:T(8,128)(2,1)}, bf16[32,4,48,256]{3,2,1,0:T(8,128)(2,1)}) custom-call(bf16[1536,1536]{1,0:T(8,128)(2,1)} %copy.24.a.table_ref, bf16[1536,1536]{1,0:T(8,128)(2,1)} %convert_element_type.33.b.turned_ref, bf16[32,4,48,256]{3,2,1,0:T(8,128)(2,1)} %copy-done.2, ...), custom_call_target="tpu_custom_call", output_to_operand_aliasing={{0}: (3, {})} | custom-call | flops 9663676416 | bytes 20000000 | tf_op jit(solution)/shard_map/fourier_step/pallas_call | solution.py:143
  495.1 193.0 %all-to-all-done.5 = bf16[32,12,48,256]{3,2,1,0:T(8,128)(2,1)} async-done(((bf16[32,12,48,256]{3,2,1,0:T(8,128)(2,1)}), bf16[32,12,48,256]{3,2,1,0:T(8,128)(2,1)}, u32[]{:S(2)}, u32[]{:S(2)}) %all-to-all-start.5) | async-done | bytes 9437216 | tf_op jit(solution)/shard_map/all_to_all | solution.py:275
  688.1 2.8 all-to-all-start.4
  690.9 0.1 reshape.208
  691.2 0.1 broadcast_in_dim.19
  691.3 0.1 broadcast_in_dim.17
  691.4 0.1 broadcast_in_dim.15
  691.5 0.7 broadcast_in_dim.20.gauss_ref
  692.2 14.5 %direct_legendre.3.rest_0_ = f32[84,128,256]{2,1,0:T(8,128)} custom-call(s32[12]{0:T(128)} %owners_ref.11, bf16[84,128,128]{2,1,0:T(8,128)(2,1)} %get-tuple-element.38.leg_ref, f32[128,128]{1,0:T(8,128)} %broadcast_in_dim.20.gauss_ref, bf16[128,48,256]{2,1,0:T(8,128)(2,1)} %bitcast.10), custom_call_target="tpu_custom_call" | custom-call | flops 5120000000 | bytes 37800000 | tf_op jit(solution)/shard_map/direct_legendre/pallas_call | solution.py:224
  706.7 0.8 broadcast_in_dim.18.gauss_ref
  707.5 24.0 %direct_legendre.4.rest_0_ = f32[84,128,256]{2,1,0:T(8,128)} custom-call(s32[12]{0:T(128)} %owners_ref.11, bf16[84,128,384]{2,1,0:T(8,128)(2,1)} %get-tuple-element.36.leg_ref, f32[384,128]{1,0:T(8,128)} %broadcast_in_dim.18.gauss_ref, bf16[384,48,256]{2,1,0:T(8,128)(2,1)} %bitcast.5.got_ref, ...), custom_call_target="tpu_custom_call", output_to_operand_aliasing={{}: (4, {})} | custom-call | flops 15360000000 | bytes 63400000 | tf_op jit(solution)/shard_map/direct_legendre/pallas_call | solution.py:224
  731.5 30.9 %all-to-all-done.4 = bf16[32,4,48,256]{3,2,1,0:T(8,128)(2,1)S(1)} async-done(((bf16[32,4,48,256]{3,2,1,0:T(8,128)(2,1)}), bf16[32,4,48,256]{3,2,1,0:T(8,128)(2,1)S(1)}, u32[]{:S(2)}, u32[]{:S(2)}) %all-to-all-start.4) | async-done | bytes 3145760 | tf_op jit(solution)/shard_map/all_to_all | solution.py:275
  762.4 0.8 broadcast_in_dim.16.gauss_ref
  763.2 0.9 copy-done
  764.1 15.6 %direct_legendre.5 = bf16[84,128,256]{2,1,0:T(8,128)(2,1)} custom-call(s32[12]{0:T(128)} %owners_ref.11, bf16[84,128,128]{2,1,0:T(8,128)(2,1)} %get-tuple-element.34.leg_ref, f32[128,128]{1,0:T(8,128)} %broadcast_in_dim.16.gauss_ref, bf16[128,48,256]{2,1,0:T(8,128)(2,1)} %bitcast.8, f32[84,128,256]{2,1,0:T(8,128)} %direct_legendre.4.rest_0_), custom_call_target="tpu_custom_call" | custom-call | flops 5120000000 | bytes 37800000 | tf_op jit(solution)/shard_map/direct_legendre/pallas_call | solution.py:224
  (18 shorter events, 0.4 us)
Async XLA Ops:
  1.9 28.1 %all-to-all-start = ((s32[32,1,12]{2,1,0:T(1,128)}), s32[32,1,12]{2,1,0:T(1,128)S(1)}, u32[]{:S(2)}, u32[]{:S(2)}) async-start(s32[32,1,12]{2,1,0:T(1,128)} %broadcast_in_dim.14), calls=%async_computation | async-start | bytes 32768 | tf_op jit(solution)/shard_map/all_to_all | solution.py:272
  31.3 77.3 %all-to-all-start.1 = ((bf16[32,4,48,256]{3,2,1,0:T(8,128)(2,1)}), bf16[32,4,48,256]{3,2,1,0:T(8,128)(2,1)S(1)}, u32[]{:S(2)}, u32[]{:S(2)}) async-start(bf16[32,4,48,256]{3,2,1,0:T(8,128)(2,1)} %bitcast.11), calls=%async_computation.1 | async-start | bytes 6291456 | tf_op jit(solution)/shard_map/all_to_all | solution.py:275
  108.6 1.6 copy-start.1
  110.2 213.3 %all-to-all-start.2 = ((bf16[32,12,48,256]{3,2,1,0:T(8,128)(2,1)}), bf16[32,12,48,256]{3,2,1,0:T(8,128)(2,1)}, u32[]{:S(2)}, u32[]{:S(2)}) async-start(bf16[32,12,48,256]{3,2,1,0:T(8,128)(2,1)} %bitcast.9), calls=%async_computation.2 | async-start | bytes 18874368 | tf_op jit(solution)/shard_map/all_to_all | solution.py:275
  398.2 75.2 %all-to-all-start.3 = ((bf16[32,4,48,256]{3,2,1,0:T(8,128)(2,1)}), bf16[32,4,48,256]{3,2,1,0:T(8,128)(2,1)S(1)}, u32[]{:S(2)}, u32[]{:S(2)}) async-start(bf16[32,4,48,256]{3,2,1,0:T(8,128)(2,1)} %bitcast.2), calls=%async_computation.3 | async-start | bytes 6291456 | tf_op jit(solution)/shard_map/all_to_all | solution.py:275
  473.4 1.6 copy-start.2
  475.0 213.1 %all-to-all-start.5 = ((bf16[32,12,48,256]{3,2,1,0:T(8,128)(2,1)}), bf16[32,12,48,256]{3,2,1,0:T(8,128)(2,1)}, u32[]{:S(2)}, u32[]{:S(2)}) async-start(bf16[32,12,48,256]{3,2,1,0:T(8,128)(2,1)} %get-tuple-element.37), calls=%async_computation.5 | async-start | bytes 18874368 | tf_op jit(solution)/shard_map/all_to_all | solution.py:275
  495.1 195.8 %copy-start.3 = (f32[640]{0:T(1024)S(1)}, f32[640]{0:T(1024)}, u32[]{:S(2)}) copy-start(f32[640]{0:T(1024)} %param.7) | copy-start | bytes 7684
  688.1 74.3 %all-to-all-start.4 = ((bf16[32,4,48,256]{3,2,1,0:T(8,128)(2,1)}), bf16[32,4,48,256]{3,2,1,0:T(8,128)(2,1)S(1)}, u32[]{:S(2)}, u32[]{:S(2)}) async-start(bf16[32,4,48,256]{3,2,1,0:T(8,128)(2,1)} %get-tuple-element.35), calls=%async_computation.4 | async-start | bytes 6291456 | tf_op jit(solution)/shard_map/all_to_all | solution.py:275
  762.4 1.7 copy-start

commit v3 on v2

--- a/solution.py
+++ b/solution.py
@@ -40,10 +40,10 @@
     firsts, seconds = [], []
     for j in range(nbp):
         s = spec_ref[j].astype(F32)
-        lead, live = block_facts(p, j, nb, bs, m_count, s.shape)
+        lead, live = block_facts(p, j, nb, bs, m_count, (bs, 1))
         one = lead.astype(F32)
-        s = jnp.where(live, s, 0.0)
-        both = jnp.concatenate([s * one, s * (1.0 - one)], axis=1).astype(BF)
+        keep = live.astype(F32)
+        both = jnp.concatenate([s * (keep * one), s * (keep * (1.0 - one))], axis=1).astype(BF)
         firsts.append(both[:half])
         seconds.append(both[half:])
     picked = dot(leg_ref[...].reshape(nbp * bs, leg_ref.shape[2]), order_ref[...], ((1,), (0,))).astype(BF)
@@ -194,13 +194,13 @@
     for j in range(nbp):
         both = jnp.concatenate([even[j * half:(j + 1) * half], odd[j * half:(j + 1) * half]], axis=0)
         shape = (bs, 2 * chan)
-        lead, live = block_facts(p, j, nb, bs, m_count, shape)
+        lead, live = block_facts(p, j, nb, bs, m_count, (bs, 1))
         one = lead.astype(jnp.int32)
         pick = jnp.where(jnp.broadcast_to(one, shape) == 1, both[:, :2 * chan], both[:, 2 * chan:])
         if not first:
             pick = pick + prev_ref[j]
         if last:
-            pick = jnp.where(live, pick, 0.0)
+            pick = pick * live.astype(F32)
         out_ref[j] = pick.astype(out_ref.dtype)
 
 

time: 782 us -> 782 us (level)
  no operation moved by 1% of the time
where the time goes in v3:
time: 782 us; the launch traced here: 780 us
  waiting for transfers between devices  419 us (54%)
  Pallas kernels  194 us (25%)
  blocking collectives  74.7 us (10%)
  local copies, waits for them, and re-layouts  36.2 us (5%)
  starting transfers between devices  27.9 us (4%)
  other arithmetic  26.6 us (3%)
    all_to_all x5, waiting for transfers between devices, swap(): return lax.all_to_all(x, 'lat', split_axis=0, concat_axis=0, tiled=True)  419 us
    all_to_all x1, blocking collectives, swap(): return lax.all_to_all(x, 'lat', split_axis=0, concat_axis=0, tiled=True)  74.7 us
    pallas_call x3, Pallas kernels, fourier(): pl.pallas_call(kernel, grid=(lats,), in_specs=in_specs, out_specs=[pl.Blo...  70.8 us
    pallas_call x3, Pallas kernels, inverse(): pl.pallas_call(functools.partial(inverse_kernel, dims), grid_spec=pltpu.P...  69.3 us
    pallas_call x3, Pallas kernels, direct(): pl.pallas_call(functools.partial(direct_kernel, dims, prev is None, last)...  54.2 us
    all_to_all x5, starting transfers between devices, swap(): return lax.all_to_all(x, 'lat', split_axis=0, concat_axis=0, tiled=True)  20.6 us
    convert_element_type x2, local copies, waits for them, and re-layouts, fourier_basis(): return scaled.astype(BF).reshape(2 * m_count, nlon)  20 us
    cos x1, other arithmetic, fourier_basis(): jnp.cos(angles)  19.7 us
  transfers between devices with their start and end apart: 6, of which 5 were waited for; matrix products, arithmetic and copies ran while one was open for 7% of the time, Pallas kernels for 23%

profile of v3, /device:TPU:0, one launch (start us, length us, event | category | flops | bytes accessed | tf_op | source)
XLA Modules:
  0.0 779.8 jit_solution(3315614186264389748)
XLA Ops:
  0.6 1.3 broadcast_in_dim.14
  1.9 7.3 all-to-all-start
  9.3 0.1 add.102
  9.4 0.7 fusion.8.order_ref
  10.1 19.9 %inverse_legendre.3 = (bf16[128,48,256]{2,1,0:T(8,128)(2,1)}, bf16[84,128,128]{2,1,0:T(8,128)(2,1)}) custom-call(s32[12]{0:T(128)} %owners_ref.11, bf16[84,128,640]{2,1,0:T(8,128)(2,1)} %leg_ref.5, bf16[84,128,256]{2,1,0:T(8,128)(2,1)} %spec_ref.5, bf16[640,128]{1,0:T(8,128)(2,1)} %fusion.8.order_ref), custom_call_target="tpu_custom_call" | custom-call | flops 11520000000 | bytes 32800000 | tf_op jit(solution)/shard_map/inverse_legendre/pallas_call | solution.py:75
  30.0 0.5 broadcast.139
  30.6 0.7 reduce.3
  31.2 0.1 reshape.205
  31.4 5.8 all-to-all-start.1
  37.3 0.1 add.115
  37.4 0.9 fusion.7.order_ref
  38.3 29.5 %inverse_legendre.5 = (bf16[384,48,256]{2,1,0:T(8,128)(2,1)}, bf16[84,128,384]{2,1,0:T(8,128)(2,1)}) custom-call(s32[12]{0:T(128)} %owners_ref.11, bf16[84,128,640]{2,1,0:T(8,128)(2,1)} %leg_ref.5, bf16[84,128,256]{2,1,0:T(8,128)(2,1)} %spec_ref.5, bf16[640,384]{1,0:T(8,128)(2,1)} %fusion.7.order_ref), custom_call_target="tpu_custom_call" | custom-call | flops 34560000000 | bytes 58400000 | tf_op jit(solution)/shard_map/inverse_legendre/pallas_call | solution.py:75
  67.8 40.8 %all-to-all-done.1.c = bf16[32,4,48,256]{3,2,1,0:T(8,128)(2,1)S(1)} async-done(((bf16[32,4,48,256]{3,2,1,0:T(8,128)(2,1)}), bf16[32,4,48,256]{3,2,1,0:T(8,128)(2,1)S(1)}, u32[]{:S(2)}, u32[]{:S(2)}) %all-to-all-start.1) | async-done | bytes 3145760 | tf_op jit(solution)/shard_map/all_to_all | solution.py:275
  108.7 1.6 copy-done.1
  110.3 4.2 all-to-all-start.2
  114.6 0.1 add.109
  114.7 0.7 fusion.9.order_ref
  115.4 19.9 %inverse_legendre.4 = (bf16[128,48,256]{2,1,0:T(8,128)(2,1)}, bf16[84,128,128]{2,1,0:T(8,128)(2,1)}) custom-call(s32[12]{0:T(128)} %owners_ref.11, bf16[84,128,640]{2,1,0:T(8,128)(2,1)} %leg_ref.5, bf16[84,128,256]{2,1,0:T(8,128)(2,1)} %spec_ref.5, bf16[640,128]{1,0:T(8,128)(2,1)} %fusion.9.order_ref), custom_call_target="tpu_custom_call" | custom-call | flops 11520000000 | bytes 32800000 | tf_op jit(solution)/shard_map/inverse_legendre/pallas_call | solution.py:75
  135.4 0.1 copy.20
  135.5 0.1 mul.73
  135.7 19.7 %fusion.5 = (f32[768,1,1536]{2,0,1:T(8,128)S(1)}, f32[768,1,1536]{2,0,1:T(8,128)S(1)}) fusion(s32[768]{0:T(1024)S(1)} %mul.73), kind=kLoop, calls=%fused_computation.9 | loop fusion | flops 11796480 | bytes 9440256 | tf_op jit(solution)/shard_map/cos | solution.py:247
  155.4 3.6 fusion
  158.9 9.4 %copy.21 = bf16[768,2,1536]{2,1,0:T(2,128)(2,1)} copy(bf16[768,2,1536]{2,0,1:T(8,128)(2,1)} %fusion) | data formatting | bytes 9437184 | tf_op jit(solution)/shard_map/convert_element_type | solution.py:248
  168.3 10.7 %convert_element_type.33.b.turned_ref = bf16[1536,1536]{1,0:T(8,128)(2,1)} reshape(bf16[768,2,1536]{2,1,0:T(2,128)(2,1)} %copy.21) | data formatting | bytes 9437184 | tf_op jit(solution)/shard_map/convert_element_type | solution.py:248
  179.0 6.6 copy.24.a.table_ref
  185.6 16.1 %fourier_step.3 = (bf16[20,2,1536,128]{3,2,1,0:T(8,128)(2,1)}, bf16[32,4,48,256]{3,2,1,0:T(8,128)(2,1)}) custom-call(bf16[1536,1536]{1,0:T(8,128)(2,1)} %copy.24.a.table_ref, bf16[1536,1536]{1,0:T(8,128)(2,1)} %convert_element_type.33.b.turned_ref, bf16[32,4,48,256]{3,2,1,0:T(8,128)(2,1)} %copy-done.1), custom_call_target="tpu_custom_call" | custom-call | flops 9663676416 | bytes 20000000 | tf_op jit(solution)/shard_map/fourier_step/pallas_call | solution.py:143
  201.7 121.9 %all-to-all-done.2.recv_ref = bf16[32,12,48,256]{3,2,1,0:T(8,128)(2,1)} async-done(((bf16[32,12,48,256]{3,2,1,0:T(8,128)(2,1)}), bf16[32,12,48,256]{3,2,1,0:T(8,128)(2,1)}, u32[]{:S(2)}, u32[]{:S(2)}) %all-to-all-start.2) | async-done | bytes 9437216 | tf_op jit(solution)/shard_map/all_to_all | solution.py:275
  323.6 74.7 %all_to_all.36 = bf16[32,4,48,256]{3,2,1,0:T(8,128)(2,1)} all-to-all(bf16[32,4,48,256]{3,2,1,0:T(8,128)(2,1)} %get-tuple-element.39), channel_id=1, replica_groups=mesh['grp'=1,'lat'=32] {'lat'}, dimensions={0} | all-to-all | bytes 6291456 | tf_op jit(solution)/shard_map/all_to_all | solution.py:275
  398.3 3.8 all-to-all-start.3
  402.1 38.6 %fourier_step.4 = (bf16[20,2,1536,128]{3,2,1,0:T(8,128)(2,1)}, bf16[32,12,48,256]{3,2,1,0:T(8,128)(2,1)}) custom-call(bf16[1536,1536]{1,0:T(8,128)(2,1)} %copy.24.a.table_ref, bf16[1536,1536]{1,0:T(8,128)(2,1)} %convert_element_type.33.b.turned_ref, bf16[32,12,48,256]{3,2,1,0:T(8,128)(2,1)} %all-to-all-done.2.recv_ref, ...), custom_call_target="tpu_custom_call", output_to_operand_aliasing={{0}: (3, {})} | custom-call | flops 28991029248 | bytes 20000000 | tf_op jit(solution)/shard_map/fourier_step/pallas_call | solution.py:143
  440.7 32.7 %all-to-all-done.3.recv_ref = bf16[32,4,48,256]{3,2,1,0:T(8,128)(2,1)S(1)} async-done(((bf16[32,4,48,256]{3,2,1,0:T(8,128)(2,1)}), bf16[32,4,48,256]{3,2,1,0:T(8,128)(2,1)S(1)}, u32[]{:S(2)}, u32[]{:S(2)}) %all-to-all-start.3) | async-done | bytes 3145760 | tf_op jit(solution)/shard_map/all_to_all | solution.py:275
  473.4 1.6 copy-done.2
  475.1 3.9 all-to-all-start.5
  479.0 16.1 %fourier_step.5 = (bf16[20,2,1536,128]{3,2,1,0:T(8,128)(2,1)}, bf16[32,4,48,256]{3,2,1,0:T(8,128)(2,1)}) custom-call(bf16[1536,1536]{1,0:T(8,128)(2,1)} %copy.24.a.table_ref, bf16[1536,1536]{1,0:T(8,128)(2,1)} %convert_element_type.33.b.turned_ref, bf16[32,4,48,256]{3,2,1,0:T(8,128)(2,1)} %copy-done.2, ...), custom_call_target="tpu_custom_call", output_to_operand_aliasing={{0}: (3, {})} | custom-call | flops 9663676416 | bytes 20000000 | tf_op jit(solution)/shard_map/fourier_step/pallas_call | solution.py:143
  495.2 193.0 %all-to-all-done.5 = bf16[32,12,48,256]{3,2,1,0:T(8,128)(2,1)} async-done(((bf16[32,12,48,256]{3,2,1,0:T(8,128)(2,1)}), bf16[32,12,48,256]{3,2,1,0:T(8,128)(2,1)}, u32[]{:S(2)}, u32[]{:S(2)}) %all-to-all-start.5) | async-done | bytes 9437216 | tf_op jit(solution)/shard_map/all_to_all | solution.py:275
  688.2 2.8 all-to-all-start.4
  691.0 0.1 reshape.208
  691.2 0.1 broadcast_in_dim.19
  691.3 0.1 broadcast_in_dim.17
  691.5 0.1 broadcast_in_dim.15
  691.6 0.7 broadcast_in_dim.20.gauss_ref
  692.3 14.5 %direct_legendre.3.rest_0_ = f32[84,128,256]{2,1,0:T(8,128)} custom-call(s32[12]{0:T(128)} %owners_ref.11, bf16[84,128,128]{2,1,0:T(8,128)(2,1)} %get-tuple-element.38.leg_ref, f32[128,128]{1,0:T(8,128)} %broadcast_in_dim.20.gauss_ref, bf16[128,48,256]{2,1,0:T(8,128)(2,1)} %bitcast.10), custom_call_target="tpu_custom_call" | custom-call | flops 5120000000 | bytes 37800000 | tf_op jit(solution)/shard_map/direct_legendre/pallas_call | solution.py:224
  706.7 0.8 broadcast_in_dim.18.gauss_ref
  707.5 24.0 %direct_legendre.4.rest_0_ = f32[84,128,256]{2,1,0:T(8,128)} custom-call(s32[12]{0:T(128)} %owners_ref.11, bf16[84,128,384]{2,1,0:T(8,128)(2,1)} %get-tuple-element.36.leg_ref, f32[384,128]{1,0:T(8,128)} %broadcast_in_dim.18.gauss_ref, bf16[384,48,256]{2,1,0:T(8,128)(2,1)} %bitcast.5.got_ref, ...), custom_call_target="tpu_custom_call", output_to_operand_aliasing={{}: (4, {})} | custom-call | flops 15360000000 | bytes 63400000 | tf_op jit(solution)/shard_map/direct_legendre/pallas_call | solution.py:224
  731.6 30.9 %all-to-all-done.4 = bf16[32,4,48,256]{3,2,1,0:T(8,128)(2,1)S(1)} async-done(((bf16[32,4,48,256]{3,2,1,0:T(8,128)(2,1)}), bf16[32,4,48,256]{3,2,1,0:T(8,128)(2,1)S(1)}, u32[]{:S(2)}, u32[]{:S(2)}) %all-to-all-start.4) | async-done | bytes 3145760 | tf_op jit(solution)/shard_map/all_to_all | solution.py:275
  762.5 0.8 broadcast_in_dim.16.gauss_ref
  763.3 0.9 copy-done
  764.2 15.7 %direct_legendre.5 = bf16[84,128,256]{2,1,0:T(8,128)(2,1)} custom-call(s32[12]{0:T(128)} %owners_ref.11, bf16[84,128,128]{2,1,0:T(8,128)(2,1)} %get-tuple-element.34.leg_ref, f32[128,128]{1,0:T(8,128)} %broadcast_in_dim.16.gauss_ref, bf16[128,48,256]{2,1,0:T(8,128)(2,1)} %bitcast.8, f32[84,128,256]{2,1,0:T(8,128)} %direct_legendre.4.rest_0_), custom_call_target="tpu_custom_call" | custom-call | flops 5120000000 | bytes 37800000 | tf_op jit(solution)/shard_map/direct_legendre/pallas_call | solution.py:224
  (18 shorter events, 0.4 us)
Async XLA Ops:
  1.9 28.1 %all-to-all-start = ((s32[32,1,12]{2,1,0:T(1,128)}), s32[32,1,12]{2,1,0:T(1,128)S(1)}, u32[]{:S(2)}, u32[]{:S(2)}) async-start(s32[32,1,12]{2,1,0:T(1,128)} %broadcast_in_dim.14), calls=%async_computation | async-start | bytes 32768 | tf_op jit(solution)/shard_map/all_to_all | solution.py:272
  31.4 77.3 %all-to-all-start.1 = ((bf16[32,4,48,256]{3,2,1,0:T(8,128)(2,1)}), bf16[32,4,48,256]{3,2,1,0:T(8,128)(2,1)S(1)}, u32[]{:S(2)}, u32[]{:S(2)}) async-start(bf16[32,4,48,256]{3,2,1,0:T(8,128)(2,1)} %bitcast.11), calls=%async_computation.1 | async-start | bytes 6291456 | tf_op jit(solution)/shard_map/all_to_all | solution.py:275
  108.7 1.6 copy-start.1
  110.3 213.3 %all-to-all-start.2 = ((bf16[32,12,48,256]{3,2,1,0:T(8,128)(2,1)}), bf16[32,12,48,256]{3,2,1,0:T(8,128)(2,1)}, u32[]{:S(2)}, u32[]{:S(2)}) async-start(bf16[32,12,48,256]{3,2,1,0:T(8,128)(2,1)} %bitcast.9), calls=%async_computation.2 | async-start | bytes 18874368 | tf_op jit(solution)/shard_map/all_to_all | solution.py:275
  398.3 75.2 %all-to-all-start.3 = ((bf16[32,4,48,256]{3,2,1,0:T(8,128)(2,1)}), bf16[32,4,48,256]{3,2,1,0:T(8,128)(2,1)S(1)}, u32[]{:S(2)}, u32[]{:S(2)}) async-start(bf16[32,4,48,256]{3,2,1,0:T(8,128)(2,1)} %bitcast.2), calls=%async_computation.3 | async-start | bytes 6291456 | tf_op jit(solution)/shard_map/all_to_all | solution.py:275
  473.4 1.6 copy-start.2
  475.1 213.1 %all-to-all-start.5 = ((bf16[32,12,48,256]{3,2,1,0:T(8,128)(2,1)}), bf16[32,12,48,256]{3,2,1,0:T(8,128)(2,1)}, u32[]{:S(2)}, u32[]{:S(2)}) async-start(bf16[32,12,48,256]{3,2,1,0:T(8,128)(2,1)} %get-tuple-element.37), calls=%async_computation.5 | async-start | bytes 18874368 | tf_op jit(solution)/shard_map/all_to_all | solution.py:275
  495.2 195.8 %copy-start.3 = (f32[640]{0:T(1024)S(1)}, f32[640]{0:T(1024)}, u32[]{:S(2)}) copy-start(f32[640]{0:T(1024)} %param.7) | copy-start | bytes 7684
  688.2 74.3 %all-to-all-start.4 = ((bf16[32,4,48,256]{3,2,1,0:T(8,128)(2,1)}), bf16[32,4,48,256]{3,2,1,0:T(8,128)(2,1)S(1)}, u32[]{:S(2)}, u32[]{:S(2)}) async-start(bf16[32,4,48,256]{3,2,1,0:T(8,128)(2,1)} %get-tuple-element.35), calls=%async_computation.4 | async-start | bytes 6291456 | tf_op jit(solution)/shard_map/all_to_all | solution.py:275
  762.5 1.7 copy-start
